TPU v7x, 256 devices: a whole 4x4x8 slice. The times are simulated.
256 devices in a mesh: group: 4 (over x), tile: 32 (over z, y), video: 2 (over core).
Axes of the slice: x: 4, y: 4, z: 8, core: 2. Of those that a mesh axis runs over, the one named last changes fastest.
Arguments:
- features: bfloat16 [64, 8, 16, 24, 384], P(('video', 'tile'), 'group'), parts along dimension 0, may hold values from -6 to 6
- group_slot: int32 [4], replicated, may hold values from 0 to 3, each once
- margins: int32 [32, 4], P('tile'), may hold values from 0 to 4, as said below
- norm_gain: float32 [384], replicated, may hold values from 0.1 to 1.9
- kernel: bfloat16 [3, 3, 3, 384, 384], replicated, may hold values from -0.0625 to 0.0625
- conv_bias: float32 [384], replicated, may hold values from -3 to 3
Outputs:
- decoded: bfloat16 [64, 8, 16, 24, 384], P(('video', 'tile'), 'group'), parts along dimension 0
There are 2 independent parts, one for each index of `video`. A program takes and returns all parts, laid end to end along the dimension named above; an argument that names none is the same for every part. Nothing has to cross between parts.
Inputs may be any that keep to these rules, and one draw needn't show every extreme that they name: group_slot is a permutation of 0 to 3. margins[t] is (left, right, up, down) of tile t; a margin is 0 exactly at the image's border and 1 to 4 elsewhere; the margin a tile has toward a neighbour equals the neighbour's margin back; left and right margins depend only on the tile's column, up and down margins are the same for all columns; some margin equals 4.
All inputs are finite; a program needn't handle non-finite values.
Results may differ from a plain program's by a relative error of at most 0.0043.
Values may be sent and summed in bfloat16 or wider, within the bound.
No kernel may reach another device: no remote copies, remote signals or barrier semaphores. Data moves between devices by JAX's collectives and lax.ppermute only.
A program may use at most 128 MiB of HBM per device.

v0:
```python
import jax
import jax.numpy as jnp
from jax import lax
from jax.experimental import pallas as pl
from jax.experimental.pallas import tpu as pltpu
from jax.sharding import PartitionSpec as P

GRID_R = 2
ROWS, COLS, C = 16, 24, 384
CELLS = ROWS * COLS
PAIR = 2 * COLS
DEPTH = 9 * C


def activated(values, half_gain):
    inv_norm = lax.rsqrt(jnp.mean(values * values, axis=-1, keepdims=True) + 1e-06)
    half = values * inv_norm * half_gain
    silu = half + half * jnp.tanh(half)
    return silu.astype(jnp.bfloat16).astype(jnp.float32)


def blend_coef(position, tap, core, near, far):
    source = position + (tap - 1)
    near_f, far_f = near.astype(jnp.float32), far.astype(jnp.float32)
    weight_near = jnp.maximum(near - position, 0).astype(jnp.float32) / (near_f + 1.0)
    weight_far = jnp.maximum(far + 1 - core + position, 0).astype(jnp.float32) / (far_f + 1.0)
    kept = jnp.where(source < near, weight_near, 0.0)
    kept = kept + jnp.where(source >= core - far, weight_far, 0.0)
    kept = kept + jnp.where((source >= -near) & (source < core + far), 1.0, 0.0)
    return kept / (weight_near + 1.0 + weight_far)


def shifted(block, left, right, coef_first, coef_last):
    size = block.shape[0]
    place = lax.broadcasted_iota(jnp.int32, (8, C), 0)
    before = pltpu.roll(block, 1, 0)
    after = pltpu.roll(block, size - 1, 0)
    before_parts, after_parts = [], []
    for n in range(size // COLS):
        first, middle, last = (slice(n * COLS + at, n * COLS + at + 8) for at in (0, 8, 16))
        before_parts += [
            jnp.where(place == 0, left[n], before[first]),
            before[middle],
            before[last] * coef_first,
        ]
        after_parts += [
            after[first] * coef_last,
            after[middle],
            jnp.where(place == 7, right[n], after[last]),
        ]
    return jnp.concatenate(before_parts, axis=0), block, jnp.concatenate(after_parts, axis=0)


def expand(margins, core, gain, row_coefs, spare, stacked, columns):
    fill_row_coefs(margins, row_coefs)
    coef_first, coef_last = column_coefs(margins)
    half_gain = 0.5 * gain
    zeros = [jnp.zeros((1, C), jnp.float32)] * 4
    spare[...] = jnp.zeros_like(spare)

    def lanes(b, e):
        return slice((3 * b + e) * C, (3 * b + e + 1) * C)

    def put(f, k, b, e, values, scale):
        if scale:
            values = [
                p * row_coefs[b // 2, pl.ds(2 * k + n, 1), :] for n, p in enumerate(values)
            ]
        values = jnp.concatenate(values, axis=0).astype(jnp.bfloat16)
        stacked[f, pl.ds(pl.multiple_of(k * PAIR, 16), PAIR), lanes(b, e)] = values

    def two_rows(k, _):
        blocks = [
            core[pl.ds(pl.multiple_of(f * CELLS + k * PAIR, 16), PAIR), :].astype(jnp.float32)
            for f in range(2)
        ]
        if columns is not None:
            for f in range(2):
                for n in range(2):
                    first, last = n * COLS, n * COLS + COLS - 1
                    columns[0, f, pl.ds(2 * k + n, 1), :] = blocks[f][first : first + 1]
                    columns[1, f, pl.ds(2 * k + n, 1), :] = blocks[f][last : last + 1]
        block = activated(jnp.concatenate(blocks, axis=0), half_gain)
        views = shifted(block, zeros, zeros, coef_first, coef_last)
        for f in range(2):
            for e in range(3):
                rows = [views[e][(2 * f + n) * COLS : (2 * f + n + 1) * COLS] for n in range(2)]
                put(f, k, 1, e, rows, False)
                odd = [spare[f, e], rows[0]]
                spare[f, e] = rows[1]
                put(f, k, 0, e, odd, True)
                put(f, jnp.maximum(k - 1, 0), 2, e, odd, True)
        return 0

    lax.fori_loop(0, ROWS // 2, two_rows, 0)
    for f in range(2):
        for e in range(3):
            put(f, ROWS // 2 - 1, 2, e, [spare[f, e], jnp.zeros((COLS, C), jnp.float32)], False)


def fill_row_coefs(margins, row_coefs):
    row = lax.broadcasted_iota(jnp.int32, (ROWS, C), 0)
    for n, b in enumerate((0, 2)):
        row_coefs[n] = blend_coef(row, b, ROWS, margins[0, 2], margins[0, 3])


def column_coefs(margins):
    place = lax.broadcasted_iota(jnp.int32, (8, C), 0)
    coef_first = blend_coef(place + (COLS - 8), 0, COLS, margins[0, 0], margins[0, 1])
    coef_last = blend_coef(place, 2, COLS, margins[0, 0], margins[0, 1])
    return coef_first, coef_last


def dot(a, b):
    return jnp.dot(a, b, preferred_element_type=jnp.float32)


def weights_of(weights, times):
    return jnp.concatenate([weights[a] for a in times], axis=1)


def expand_kernel(
    margins, core, gain, weights, stacked, columns, taps, row_coefs, spare, cells, sems
):
    copies = [
        pltpu.make_async_copy(weights.at[2 - n], taps.at[:, pl.ds(n * C, C)], sems.at[n])
        for n in range(3)
    ]
    for copy in copies:
        copy.start()
    expand(margins, core, gain[...].reshape(1, C), row_coefs, spare, stacked, cells)
    columns[...] = cells[...].astype(jnp.bfloat16)
    for copy in copies:
        copy.wait()


def own_kernel(stacked, taps, own):
    third = DEPTH // 3
    own[...] = jnp.zeros_like(own)

    def part(n, _):
        rows = pl.ds(pl.multiple_of((n // 3) * 192, 16), 192)
        depth = pl.ds(pl.multiple_of((n % 3) * third, 128), third)
        both = dot(stacked[0, rows, depth], taps[depth, : 2 * C])
        own[0, rows, :] += both[:, :C]
        own[1, rows, :] += both[:, C:] + dot(stacked[1, rows, depth], taps[depth, :C])
        return 0

    lax.fori_loop(0, 3 * (CELLS // 192), part, 0)


def previous_kernel(
    margins, group_slot, group, core, gain, taps, own, bias, sums, row_coefs, spare, stacked
):
    bias = bias[...].reshape(1, C)
    gain = jnp.where(group_slot[group[0]] > 0, gain[...].reshape(1, C), 0.0)
    expand(margins, core, gain, row_coefs, spare, stacked, None)

    def part(n, _):
        rows = pl.ds(pl.multiple_of(n * 128, 16), 128)
        both = dot(stacked[1, rows, :], taps[:, C:])
        last = dot(stacked[0, rows, :], taps[:, 2 * C :])
        sums[0, rows, :] = own[0, rows, :] + bias + both[:, :C] + last
        sums[1, rows, :] = own[1, rows, :] + bias + both[:, C:]
        return 0

    lax.fori_loop(0, CELLS // 128, part, 0)


def join_kernel(
    margins,
    tile_row,
    group_slot,
    group,
    halo,
    halo_previous,
    gain,
    taps,
    sums,
    out,
    row_coefs,
    sides,
    near,
    columns,
    rims,
):
    fill_row_coefs(margins, row_coefs)
    coef_first, coef_last = column_coefs(margins)
    half_gain = 0.5 * gain[...].reshape(1, C)
    half_previous = jnp.where(group_slot[group[0]] > 0, half_gain, 0.0)
    top = tile_row[0] == 1
    none = jnp.zeros((1, C), jnp.float32)

    def frames(f, _):
        for n, (source, scale) in enumerate(((halo_previous, half_previous), (halo, half_gain))):
            rim, left, right = (
                activated(source[part, f].astype(jnp.float32), scale) for part in range(3)
            )
            views = shifted(
                rim, [left[ROWS : ROWS + 1]], [right[ROWS : ROWS + 1]], coef_first, coef_last
            )
            at = 2 * n + f
            for e in range(3):
                values = jnp.concatenate([views[e], jnp.zeros((8, C), jnp.float32)], axis=0)
                rims[e, pl.ds(pl.multiple_of(at * 32, 32), 32), :] = values.astype(jnp.bfloat16)
            for side, column in enumerate((left[:ROWS], right[:ROWS])):
                above = jnp.concatenate([none, column[: ROWS - 1]], axis=0) * row_coefs[0]
                below = jnp.concatenate([column[1:], none], axis=0) * row_coefs[1]
                for b, values in enumerate((above, column, below)):
                    rows = pl.ds(pl.multiple_of(at * ROWS, 16), ROWS)
                    columns[3 * side + b, rows, :] = values.astype(jnp.bfloat16)
        return 0

    lax.fori_loop(0, 2, frames, 0)
    sides[...] = jnp.zeros_like(sides)
    near[...] = jnp.zeros_like(near)
    first = jnp.where(top, 0, 6)

    def times(a, _):
        lanes = pl.ds(pl.multiple_of((2 - a) * C, 128), C)

        def weight(row):
            return taps[pl.ds(pl.multiple_of(row * C, 16), C), lanes]

        rows = pl.ds(pl.multiple_of(a * ROWS, 16), 2 * ROWS)
        for side in range(2):
            sides[side] += sum(
                dot(columns[3 * side + b, rows, :], weight(3 * b + 2 * side)) for b in range(3)
            )
        rows = pl.ds(pl.multiple_of(a * 32, 32), 64)
        near[...] += sum(dot(rims[e, rows, :], weight(first + e)) for e in range(3))
        return 0

    lax.fori_loop(0, 3, times, 0)
    place = lax.broadcasted_iota(jnp.int32, (8, C), 0)

    def two_rows(k, _):
        for f in range(2):
            block = sums[f, pl.ds(pl.multiple_of(k * PAIR, 16), PAIR), :]
            beside = near[32 * f : 32 * f + COLS]
            parts = []
            for n, here in enumerate((top & (k == 0), ~top & (k == ROWS // 2 - 1))):
                values = block[n * COLS : (n + 1) * COLS] + jnp.where(here, beside, 0.0)
                at = pl.ds(f * ROWS + 2 * k + n, 1)
                parts += [
                    values[:8] + jnp.where(place == 0, sides[0, at, :], 0.0),
                    values[8:16],
                    values[16:] + jnp.where(place == 7, sides[1, at, :], 0.0),
                ]
            rows = pl.ds(pl.multiple_of(f * CELLS + k * PAIR, 16), PAIR)
            out[rows, :] = jnp.concatenate(parts, axis=0).astype(jnp.bfloat16)
        return 0

    lax.fori_loop(0, ROWS // 2, two_rows, 0)


SMEM, VMEM, HBM = (pl.BlockSpec(memory_space=m) for m in (pltpu.SMEM, pltpu.VMEM, pl.ANY))
COEFS = pltpu.VMEM((2, ROWS, C), jnp.float32)
SPARE = pltpu.VMEM((2, 3, COLS, C), jnp.float32)
STACKED = pltpu.VMEM((2, CELLS, DEPTH), jnp.bfloat16)
PARTIAL = jax.ShapeDtypeStruct((2, CELLS, C), jnp.float32)


def call(kernel, inputs, specs, outputs, scratch, flops, mib):
    many = isinstance(outputs, list)
    return pl.pallas_call(
        kernel,
        in_specs=specs,
        out_specs=[VMEM] * len(outputs) if many else VMEM,
        out_shape=outputs,
        scratch_shapes=scratch,
        compiler_params=pltpu.CompilerParams(vmem_limit_bytes=mib * 2**20),
        cost_estimate=pl.CostEstimate(
            flops=flops, bytes_accessed=8 * 2**20, transcendentals=2 * CELLS * C
        ),
    )(*inputs)


def prepare_kernel(group_slot, tile_row, core, index, rim, sems):
    row = jnp.where(tile_row[0] == 1, 0, ROWS - 1)
    copies = [
        pltpu.make_async_copy(core.at[0, f, row], rim.at[f], sems.at[f]) for f in range(2)
    ]
    for copy in copies:
        copy.start()
    away = [(group_slot[d] - group_slot[0] + 4) % 4 for d in (1, 2, 3)]
    index[0] = (away[0] - 1) * 2 + jnp.where(away[1] > away[2], 1, 0)
    for copy in copies:
        copy.wait()


def prepare(group_slot, tile_row, features):
    return pl.pallas_call(
        prepare_kernel,
        in_specs=[SMEM, SMEM, HBM],
        out_specs=[SMEM, VMEM],
        out_shape=[
            jax.ShapeDtypeStruct((1,), jnp.int32),
            jax.ShapeDtypeStruct((2, COLS, C), jnp.bfloat16),
        ],
        scratch_shapes=[pltpu.SemaphoreType.DMA((2,))],
    )(group_slot, tile_row, features)


def cyclic_order(index):
    place = index // 2 + 1
    others = [p for p in (1, 2, 3) if p != place]
    if index % 2:
        others = others[::-1]
    places = [0, place] + others
    return sorted(range(4), key=lambda d: places[d])


def local(features, group_slot, margins, norm_gain, kernel, conv_bias):
    tiles = lax.axis_size("tile")
    across = tiles // GRID_R
    tile_row = (lax.axis_index("tile") // across).astype(jnp.int32).reshape(1)
    group = lax.axis_index("group").astype(jnp.int32).reshape(1)
    weights = kernel.reshape(3, DEPTH, C)
    index, edge = prepare(group_slot, tile_row, features)
    conv_flops = 2 * 3 * CELLS * DEPTH * C

    def routed(order):
        route = [(order[n], order[(n + 1) % 4]) for n in range(4)]

        def branch(features, edge, margins, tile_row, group_slot, group, gain, weights, bias):
            previous = lax.ppermute(features, "group", route)
            rim = lax.ppermute(edge, "tile", [(t, (t + across) % tiles) for t in range(tiles)])
            stacked, columns, taps = call(
                expand_kernel,
                (margins, features.reshape(2 * CELLS, C), gain, weights),
                [SMEM, VMEM, VMEM, HBM],
                [
                    jax.ShapeDtypeStruct((2, CELLS, DEPTH), jnp.bfloat16),
                    jax.ShapeDtypeStruct((2, 2, ROWS, C), jnp.bfloat16),
                    jax.ShapeDtypeStruct((DEPTH, 3 * C), jnp.bfloat16),
                ],
                [
                    COEFS,
                    SPARE,
                    pltpu.VMEM((2, 2, ROWS, C), jnp.float32),
                    pltpu.SemaphoreType.DMA((3,)),
                ],
                2 * CELLS * DEPTH,
                16,
            )
            own = call(own_kernel, (stacked, taps), [VMEM] * 2, PARTIAL, [], conv_flops, 16)
            spare = jnp.zeros((2, COLS - ROWS - 1, C), jnp.bfloat16)
            first, last = (
                jnp.concatenate([columns[side], rim[:, at : at + 1], spare], axis=1)
                for side, at in ((0, 0), (1, COLS - 1))
            )
            inner = [t for t in range(tiles) if t % across != across - 1]
            left = lax.ppermute(last, "tile", [(t, t + 1) for t in inner])
            right = lax.ppermute(first, "tile", [(t + 1, t) for t in inner])
            halo = jnp.stack([rim, left, right])
            halo_previous = lax.ppermute(halo, "group", route)
            sums = call(
                previous_kernel,
                (margins, group_slot, group, previous.reshape(2 * CELLS, C), gain, taps, own, bias),
                [SMEM, SMEM, SMEM, VMEM, VMEM, VMEM, VMEM, VMEM],
                PARTIAL,
                [COEFS, SPARE, STACKED],
                conv_flops,
                16,
            )
            return call(
                join_kernel,
                (margins, tile_row, group_slot, group, halo, halo_previous, gain, taps, sums),
                [SMEM] * 4 + [VMEM] * 5,
                jax.ShapeDtypeStruct((2 * CELLS, C), jnp.bfloat16),
                [
                    COEFS,
                    pltpu.VMEM((2, 2 * ROWS, C), jnp.float32),
                    pltpu.VMEM((64, C), jnp.float32),
                    pltpu.VMEM((6, 4 * ROWS, C), jnp.bfloat16),
                    pltpu.VMEM((3, 4 * 32, C), jnp.bfloat16),
                ],
                2 * 3 * 9 * 40 * C * C,
                16,
            )

        return branch

    decoded = lax.switch(
        index[0],
        [routed(cyclic_order(n)) for n in range(6)],
        features,
        edge,
        margins,
        tile_row,
        group_slot,
        group,
        norm_gain,
        weights,
        conv_bias,
    )
    return decoded.reshape(1, 2, ROWS, COLS, C)


def solution(mesh):
    return jax.shard_map(
        local,
        mesh=mesh,
        in_specs=(
            P(("video", "tile"), "group", None, None, None),
            P(),
            P("tile", None),
            P(),
            P(),
            P(),
        ),
        out_specs=P(("video", "tile"), "group", None, None, None),
        check_vma=False,
    )
```

profile of v0, /device:TPU:32, one launch (start us, length us, event | category | flops | bytes accessed | tf_op | source)
XLA Modules:
  0.0 41.4 jit_solution(9691756125286272555)
XLA Ops:
  0.0 1.9 %shard_map.94 = (s32[1]{0:T(128)}, bf16[2,24,384]{2,1,0:T(8,128)(2,1)S(1)}) custom-call(s32[4]{0:T(128)} %group_slot.1, s32[1]{0:T(128)} %bitcast.60.tile_row, bf16[1,2,16,24,384]{4,3,2,1,0:T(8,128)(2,1)} %core.1), custom_call_target="tpu_custom_call" | custom-call | tf_op jit(solution)/shard_map/pallas_call | solution.py:293
  2.6 37.9 %conditional.1 = (bf16[1,2,16,24,384]{4,3,2,1,0:T(8,128)(2,1)S(1)}) conditional(s32[]{:T(128)} %bitcast.61, (bf16[2,24,384]{2,1,0:T(8,128)(2,1)S(1)}, bf16[1,2,16,24,384]{4,3,2,1,0:T(8,128)(2,1)}, s32[1,4]{1,0:T(1,128)}, f32[384]{0:T(512)}, bf16[3,3,3,384,384]{4,3,2,1,0:T(8,128)(2,1)}, /*index=5*/s32[4]{0:T(128)}, ...), branch_computations={%region_0.1_spmd, %region_1.2_spmd, %region_2.3_spmd, %region_3.4_... | conditional | flops 6436767744 | bytes 37262912 | solution.py:385
  2.7 6.4 %collective-permute-start.10 = (bf16[2,24,384]{2,1,0:T(8,128)(2,1)S(1)}, bf16[2,24,384]{2,1,0:T(8,128)(2,1)S(1)}, u32[]{:S(2)}, u32[]{:S(2)}) collective-permute-start(bf16[2,24,384]{2,1,0:T(8,128)(2,1)S(1)} %get-tuple-element.149), channel_id=1, source_target_pairs={{0,32},{2,34},{4,36},{6,38},{8,40},{10,42},{12,44},{14,46},{16,48}... | collective-permute-start | bytes 110600 | tf_op jit(solution)/shard_map/cond/branch_2_fun/ppermute | solution.py:328
  9.0 3.0 %collective-permute-start.14 = (bf16[1,2,16,24,384]{4,3,2,1,0:T(8,128)(2,1)}, bf16[1,2,16,24,384]{4,3,2,1,0:T(8,128)(2,1)S(1)}, u32[]{:S(2)}, u32[]{:S(2)}) collective-permute-start(bf16[1,2,16,24,384]{4,3,2,1,0:T(8,128)(2,1)} %get-tuple-element.150), channel_id=1, source_target_pairs={{0,128},{128,64},{64,192},{192,0},{1,129},{129,65},{65,193},{193,1... | collective-permute-start | bytes 1769480 | tf_op jit(solution)/shard_map/cond/branch_2_fun/ppermute | solution.py:327
  12.1 4.5 %branch_2_fun.4 = (bf16[2,384,3456]{2,1,0:T(8,128)(2,1)S(1)}, bf16[2,2,16,384]{3,2,1,0:T(8,128)(2,1)S(1)}, bf16[3456,1152]{1,0:T(8,128)(2,1)S(1)}) custom-call(s32[1,4]{1,0:T(1,128)} %get-tuple-element.230.margins, bf16[768,384]{1,0:T(8,128)(2,1)} %bitcast.88, f32[384]{0:T(512)} %get-tuple-element.236.gain, bf16[3,3456,384]{2,1,0:T(8,128)(2,1)} %bitcast.82), custom_call_target="tpu_custom_call" | custom-call | flops 2654208 | bytes 8388608 | tf_op jit(solution)/shard_map/cond/branch_2_fun/pallas_call | solution.py:266
  16.6 0.1 pad.26.clone
  16.7 0.0 collective-permute-done.10
  16.7 0.1 maximum_maximum_fusion.4
  16.8 3.5 %collective-permute-start.11 = (bf16[2,24,384]{2,1,0:T(8,128)(2,1)S(1)}, bf16[2,24,384]{2,1,0:T(8,128)(2,1)S(1)}, u32[]{:S(2)}, u32[]{:S(2)}) collective-permute-start(bf16[2,24,384]{2,1,0:T(8,128)(2,1)S(1)} %get-tuple-element.274), channel_id=1, source_target_pairs={{0,2},{2,4},{4,6},{6,8},{8,10},{10,12},{12,14},{14,16},{16,18},{18... | collective-permute-start | bytes 110600 | tf_op jit(solution)/shard_map/cond/branch_2_fun/ppermute | solution.py:354
  20.3 4.5 %collective-permute-start.12 = (bf16[2,24,384]{2,1,0:T(8,128)(2,1)S(1)}, bf16[2,24,384]{2,1,0:T(8,128)(2,1)S(1)}, u32[]{:S(2)}, u32[]{:S(2)}) collective-permute-start(bf16[2,24,384]{2,1,0:T(8,128)(2,1)S(1)} %get-tuple-element.275), channel_id=1, source_target_pairs={{2,0},{4,2},{6,4},{8,6},{10,8},{12,10},{14,12},{16,14},{18,16},{20... | collective-permute-start | bytes 110600 | tf_op jit(solution)/shard_map/cond/branch_2_fun/ppermute | solution.py:355
  24.7 0.0 copy-start.3
  24.7 0.0 copy-start.9
  24.8 0.0 copy-start.15
  24.8 0.0 copy-start.21
  24.8 5.0 %branch_2_fun.5.own = f32[2,384,384]{2,1,0:T(8,128)S(1)} custom-call(bf16[2,384,3456]{2,1,0:T(8,128)(2,1)S(1)} %get-tuple-element.155.stacked, bf16[3456,1152]{1,0:T(8,128)(2,1)S(1)} %get-tuple-element.154.taps), custom_call_target="tpu_custom_call" | custom-call | flops 3057647616 | bytes 8388608 | tf_op jit(solution)/shard_map/cond/branch_2_fun/pallas_call | solution.py:266
  29.8 0.0 collective-permute-done.11
  29.8 0.0 collective-permute-done.12
  29.8 0.6 %collective-permute-start.13 = (bf16[3,2,24,384]{3,2,1,0:T(8,128)(2,1)S(1)}, bf16[3,2,24,384]{3,2,1,0:T(8,128)(2,1)S(1)}, u32[]{:S(2)}, u32[]{:S(2)}) collective-permute-start(bf16[3,2,24,384]{3,2,1,0:T(8,128)(2,1)S(1)} %pad_maximum_fusion.2.halo), channel_id=1, source_target_pairs={{0,128},{128,64},{64,192},{192,0},{1,129},{129,65},{65,193},{193,1... | collective-permute-start | bytes 331784 | tf_op jit(solution)/shard_map/cond/branch_2_fun/ppermute | solution.py:357
  30.4 0.0 collective-permute-done.14
  30.5 6.7 %branch_2_fun.6.sums = f32[2,384,384]{2,1,0:T(8,128)S(1)} custom-call(s32[1,4]{1,0:T(1,128)S(1)} %copy-done.9, s32[4]{0:T(128)S(1)} %copy-done.15, s32[1]{0:T(128)} %bitcast.20.group, bf16[768,384]{1,0:T(8,128)(2,1)S(1)} %bitcast.76, f32[384]{0:T(512)S(1)} %copy-done.3, bf16[3456,1152]{1,0:T(8,128)(2,1)S(1)} %get-tuple-element.154.taps, ...), custom_call_target="tpu_custom_call" | custom-call | flops 3057647616 | bytes 8388608 | tf_op jit(solution)/shard_map/cond/branch_2_fun/pallas_call | solution.py:266
  37.2 0.0 collective-permute-done.13.halo_previous
  37.2 2.8 %branch_2_fun.7 = bf16[768,384]{1,0:T(8,128)(2,1)S(1)} custom-call(s32[1,4]{1,0:T(1,128)S(1)} %copy-done.9, s32[1]{0:T(128)} %get-tuple-element.146.tile_row, s32[4]{0:T(128)S(1)} %copy-done.15, s32[1]{0:T(128)} %bitcast.20.group, bf16[3,2,24,384]{3,2,1,0:T(8,128)(2,1)S(1)} %pad_maximum_fusion.2.halo, ...), custom_call_target="tpu_custom_call" | custom-call | flops 318504960 | bytes 8388608 | tf_op jit(solution)/shard_map/cond/branch_2_fun/pallas_call | solution.py:266
  40.5 0.0 copy-start
  40.5 0.8 %copy-done = bf16[1,2,16,24,384]{4,3,2,1,0:T(8,128)(2,1)} copy-done((bf16[1,2,16,24,384]{4,3,2,1,0:T(8,128)(2,1)}, bf16[1,2,16,24,384]{4,3,2,1,0:T(8,128)(2,1)S(1)}, u32[]{:S(2)}) %copy-start) | copy-done | bytes 589848
  (8 shorter events, 0.0 us)
Async XLA Ops:
  2.7 14.0 %collective-permute-start.10 = (bf16[2,24,384]{2,1,0:T(8,128)(2,1)S(1)}, bf16[2,24,384]{2,1,0:T(8,128)(2,1)S(1)}, u32[]{:S(2)}, u32[]{:S(2)}) collective-permute-start(bf16[2,24,384]{2,1,0:T(8,128)(2,1)S(1)} %get-tuple-element.149), channel_id=1, source_target_pairs={{0,32},{2,34},{4,36},{6,38},{8,40},{10,42},{12,44},{14,46},{16,48}... | collective-permute-start | bytes 110600 | tf_op jit(solution)/shard_map/cond/branch_2_fun/ppermute | solution.py:328
  9.0 21.4 %collective-permute-start.14 = (bf16[1,2,16,24,384]{4,3,2,1,0:T(8,128)(2,1)}, bf16[1,2,16,24,384]{4,3,2,1,0:T(8,128)(2,1)S(1)}, u32[]{:S(2)}, u32[]{:S(2)}) collective-permute-start(bf16[1,2,16,24,384]{4,3,2,1,0:T(8,128)(2,1)} %get-tuple-element.150), channel_id=1, source_target_pairs={{0,128},{128,64},{64,192},{192,0},{1,129},{129,65},{65,193},{193,1... | collective-permute-start | bytes 1769480 | tf_op jit(solution)/shard_map/cond/branch_2_fun/ppermute | solution.py:327
  16.8 13.0 %collective-permute-start.11 = (bf16[2,24,384]{2,1,0:T(8,128)(2,1)S(1)}, bf16[2,24,384]{2,1,0:T(8,128)(2,1)S(1)}, u32[]{:S(2)}, u32[]{:S(2)}) collective-permute-start(bf16[2,24,384]{2,1,0:T(8,128)(2,1)S(1)} %get-tuple-element.274), channel_id=1, source_target_pairs={{0,2},{2,4},{4,6},{6,8},{8,10},{10,12},{12,14},{14,16},{16,18},{18... | collective-permute-start | bytes 110600 | tf_op jit(solution)/shard_map/cond/branch_2_fun/ppermute | solution.py:354
  20.3 9.5 %collective-permute-start.12 = (bf16[2,24,384]{2,1,0:T(8,128)(2,1)S(1)}, bf16[2,24,384]{2,1,0:T(8,128)(2,1)S(1)}, u32[]{:S(2)}, u32[]{:S(2)}) collective-permute-start(bf16[2,24,384]{2,1,0:T(8,128)(2,1)S(1)} %get-tuple-element.275), channel_id=1, source_target_pairs={{2,0},{4,2},{6,4},{8,6},{10,8},{12,10},{14,12},{16,14},{18,16},{20... | collective-permute-start | bytes 110600 | tf_op jit(solution)/shard_map/cond/branch_2_fun/ppermute | solution.py:355
  24.7 5.7 %copy-start.3 = (f32[384]{0:T(512)S(1)}, f32[384]{0:T(512)}, u32[]{:S(2)}) copy-start(f32[384]{0:T(512)} %get-tuple-element.236.gain) | copy-start | bytes 4612 | tf_op jit(solution)/shard_map/cond
  24.7 5.7 %copy-start.9 = (s32[1,4]{1,0:T(1,128)S(1)}, s32[1,4]{1,0:T(1,128)}, u32[]{:S(2)}) copy-start(s32[1,4]{1,0:T(1,128)} %get-tuple-element.230.margins) | copy-start | bytes 52 | tf_op jit(solution)/shard_map/cond
  24.8 5.7 %copy-start.15 = (s32[4]{0:T(128)S(1)}, s32[4]{0:T(128)}, u32[]{:S(2)}) copy-start(s32[4]{0:T(128)} %get-tuple-element.147.group_slot) | copy-start | bytes 52 | tf_op jit(solution)/shard_map/cond
  24.8 5.7 %copy-start.21 = (f32[384]{0:T(512)S(1)}, f32[384]{0:T(512)}, u32[]{:S(2)}) copy-start(f32[384]{0:T(512)} %get-tuple-element.248.bias) | copy-start | bytes 4612 | tf_op jit(solution)/shard_map/cond
  29.8 7.4 %collective-permute-start.13 = (bf16[3,2,24,384]{3,2,1,0:T(8,128)(2,1)S(1)}, bf16[3,2,24,384]{3,2,1,0:T(8,128)(2,1)S(1)}, u32[]{:S(2)}, u32[]{:S(2)}) collective-permute-start(bf16[3,2,24,384]{3,2,1,0:T(8,128)(2,1)S(1)} %pad_maximum_fusion.2.halo), channel_id=1, source_target_pairs={{0,128},{128,64},{64,192},{192,0},{1,129},{129,65},{65,193},{193,1... | collective-permute-start | bytes 331784 | tf_op jit(solution)/shard_map/cond/branch_2_fun/ppermute | solution.py:357
  40.5 0.8 %copy-start = (bf16[1,2,16,24,384]{4,3,2,1,0:T(8,128)(2,1)}, bf16[1,2,16,24,384]{4,3,2,1,0:T(8,128)(2,1)S(1)}, u32[]{:S(2)}) copy-start(bf16[1,2,16,24,384]{4,3,2,1,0:T(8,128)(2,1)S(1)} %get-tuple-element.324) | copy-start | bytes 1769476
where the time goes:
time: 41.6 us; the launch traced here: 41.4 us
  Pallas kernels  20.9 us (50%)
  starting transfers between devices  18 us (43%)
  local copies, waits for them, and re-layouts  0.93 us (2%)
  loops' own time  0.71 us (2%)
  between operations  0.71 us (2%)
    pallas_call x4, Pallas kernels, call(): pl.pallas_call(kernel, in_specs=specs, out_specs=[VMEM] * len(outputs) if...  19 us
    ppermute x1, starting transfers between devices, branch(): lax.ppermute(edge, 'tile', [(t, (t + across) % tiles) for t in range(tile...  6.38 us
    ppermute x1, starting transfers between devices, branch(): right = lax.ppermute(first, 'tile', [(t + 1, t) for t in inner])  4.47 us
    ppermute x1, starting transfers between devices, branch(): left = lax.ppermute(last, 'tile', [(t, t + 1) for t in inner])  3.48 us
    ppermute x1, starting transfers between devices, branch(): previous = lax.ppermute(features, 'group', route)  3.02 us
    pallas_call x1, Pallas kernels, prepare(): pl.pallas_call(prepare_kernel, in_specs=[SMEM, SMEM, HBM], out_specs=[SME...  1.94 us
  transfers between devices with their start and end apart: 5, of which 0 were waited for; matrix products, arithmetic and copies ran while one was open for 0% of the time, Pallas kernels for 39%

commit v1 on v0

--- a/solution.py
+++ b/solution.py
@@ -51,7 +51,7 @@
     return jnp.concatenate(before_parts, axis=0), block, jnp.concatenate(after_parts, axis=0)
 
 
-def expand(margins, core, gain, row_coefs, spare, stacked, columns):
+def expand(margins, core, gain, row_coefs, spare, ahead, stacked, columns):
     fill_row_coefs(margins, row_coefs)
     coef_first, coef_last = column_coefs(margins)
     half_gain = 0.5 * gain
@@ -67,20 +67,25 @@
                 p * row_coefs[b // 2, pl.ds(2 * k + n, 1), :] for n, p in enumerate(values)
             ]
         values = jnp.concatenate(values, axis=0).astype(jnp.bfloat16)
-        stacked[f, pl.ds(pl.multiple_of(k * PAIR, 16), PAIR), lanes(b, e)] = values
-
-    def two_rows(k, _):
+        stacked[f][pl.ds(pl.multiple_of(k * PAIR, 16), PAIR), lanes(b, e)] = values
+
+    ahead[...] = jnp.zeros_like(ahead)
+
+    def two_rows(step, _):
+        block = ahead[...]
+        after = jnp.minimum(step, ROWS // 2 - 1)
         blocks = [
-            core[pl.ds(pl.multiple_of(f * CELLS + k * PAIR, 16), PAIR), :].astype(jnp.float32)
+            core[pl.ds(pl.multiple_of(f * CELLS + after * PAIR, 16), PAIR), :].astype(jnp.float32)
             for f in range(2)
         ]
         if columns is not None:
             for f in range(2):
                 for n in range(2):
                     first, last = n * COLS, n * COLS + COLS - 1
-                    columns[0, f, pl.ds(2 * k + n, 1), :] = blocks[f][first : first + 1]
-                    columns[1, f, pl.ds(2 * k + n, 1), :] = blocks[f][last : last + 1]
-        block = activated(jnp.concatenate(blocks, axis=0), half_gain)
+                    columns[0, f, pl.ds(2 * after + n, 1), :] = blocks[f][first : first + 1]
+                    columns[1, f, pl.ds(2 * after + n, 1), :] = blocks[f][last : last + 1]
+        ahead[...] = activated(jnp.concatenate(blocks, axis=0), half_gain)
+        k = jnp.maximum(step - 1, 0)
         views = shifted(block, zeros, zeros, coef_first, coef_last)
         for f in range(2):
             for e in range(3):
@@ -92,7 +97,7 @@
                 put(f, jnp.maximum(k - 1, 0), 2, e, odd, True)
         return 0
 
-    lax.fori_loop(0, ROWS // 2, two_rows, 0)
+    lax.fori_loop(0, ROWS // 2 + 1, two_rows, 0)
     for f in range(2):
         for e in range(3):
             put(f, ROWS // 2 - 1, 2, e, [spare[f, e], jnp.zeros((COLS, C), jnp.float32)], False)
@@ -119,8 +124,33 @@
     return jnp.concatenate([weights[a] for a in times], axis=1)
 
 
-def expand_kernel(
-    margins, core, gain, weights, stacked, columns, taps, row_coefs, spare, cells, sems
+def add_products(to, rows_of, weights_of):
+    third = DEPTH // 3
+
+    def part(n, _):
+        rows = pl.ds(pl.multiple_of((n // 3) * 192, 16), 192)
+        depth = pl.ds(pl.multiple_of((n % 3) * third, 128), third)
+        to(rows, dot(rows_of(rows, depth), weights_of(depth)))
+        return 0
+
+    lax.fori_loop(0, 3 * (CELLS // 192), part, 0)
+
+
+def expand_own_kernel(
+    margins,
+    core,
+    gain,
+    weights,
+    early,
+    own,
+    columns,
+    taps,
+    row_coefs,
+    spare,
+    ahead,
+    cells,
+    late,
+    sems,
 ):
     copies = [
         pltpu.make_async_copy(weights.at[2 - n], taps.at[:, pl.ds(n * C, C)], sems.at[n])
@@ -128,33 +158,39 @@
     ]
     for copy in copies:
         copy.start()
-    expand(margins, core, gain[...].reshape(1, C), row_coefs, spare, stacked, cells)
+    own[...] = jnp.zeros_like(own)
+    expand(margins, core, gain[...].reshape(1, C), row_coefs, spare, ahead, (early, late), cells)
     columns[...] = cells[...].astype(jnp.bfloat16)
-    for copy in copies:
+    copies[0].wait()
+
+    def add(rows, product):
+        own[rows, :] += product
+
+    add_products(add, lambda rows, depth: late[rows, depth], lambda depth: taps[depth, :C])
+    for copy in copies[1:]:
         copy.wait()
 
 
-def own_kernel(stacked, taps, own):
-    third = DEPTH // 3
-    own[...] = jnp.zeros_like(own)
-
-    def part(n, _):
-        rows = pl.ds(pl.multiple_of((n // 3) * 192, 16), 192)
-        depth = pl.ds(pl.multiple_of((n % 3) * third, 128), third)
-        both = dot(stacked[0, rows, depth], taps[depth, : 2 * C])
-        own[0, rows, :] += both[:, :C]
-        own[1, rows, :] += both[:, C:] + dot(stacked[1, rows, depth], taps[depth, :C])
-        return 0
-
-    lax.fori_loop(0, 3 * (CELLS // 192), part, 0)
-
-
-def previous_kernel(
-    margins, group_slot, group, core, gain, taps, own, bias, sums, row_coefs, spare, stacked
+def own_kernel(early, taps, late, own):
+    own[0] = jnp.zeros_like(late)
+    own[1] = late[...]
+
+    def add(rows, product):
+        own[0, rows, :] += product[:, :C]
+        own[1, rows, :] += product[:, C:]
+
+    add_products(add, lambda rows, depth: early[rows, depth], lambda depth: taps[depth, : 2 * C])
+
+
+def expand_previous_kernel(
+    margins, group_slot, group, core, gain, stacked, row_coefs, spare, ahead
 ):
+    gain = jnp.where(group_slot[group[0]] > 0, gain[...].reshape(1, C), 0.0)
+    expand(margins, core, gain, row_coefs, spare, ahead, (stacked.at[0], stacked.at[1]), None)
+
+
+def previous_kernel(stacked, taps, own, bias, sums):
     bias = bias[...].reshape(1, C)
-    gain = jnp.where(group_slot[group[0]] > 0, gain[...].reshape(1, C), 0.0)
-    expand(margins, core, gain, row_coefs, spare, stacked, None)
 
     def part(n, _):
         rows = pl.ds(pl.multiple_of(n * 128, 16), 128)
@@ -257,7 +293,7 @@
 SMEM, VMEM, HBM = (pl.BlockSpec(memory_space=m) for m in (pltpu.SMEM, pltpu.VMEM, pl.ANY))
 COEFS = pltpu.VMEM((2, ROWS, C), jnp.float32)
 SPARE = pltpu.VMEM((2, 3, COLS, C), jnp.float32)
-STACKED = pltpu.VMEM((2, CELLS, DEPTH), jnp.bfloat16)
+AHEAD = pltpu.VMEM((2 * PAIR, C), jnp.float32)
 PARTIAL = jax.ShapeDtypeStruct((2, CELLS, C), jnp.float32)
 
 
@@ -271,35 +307,36 @@
         scratch_shapes=scratch,
         compiler_params=pltpu.CompilerParams(vmem_limit_bytes=mib * 2**20),
         cost_estimate=pl.CostEstimate(
-            flops=flops, bytes_accessed=8 * 2**20, transcendentals=2 * CELLS * C
+            flops=flops, bytes_accessed=flops // 2**10, transcendentals=0
         ),
     )(*inputs)
 
 
-def prepare_kernel(group_slot, tile_row, core, index, rim, sems):
+def prepare_kernel(core, group_slot, tile_row, index, rim, slots, sems):
     row = jnp.where(tile_row[0] == 1, 0, ROWS - 1)
-    copies = [
+    copies = [pltpu.make_async_copy(group_slot, slots, sems.at[2])] + [
         pltpu.make_async_copy(core.at[0, f, row], rim.at[f], sems.at[f]) for f in range(2)
     ]
     for copy in copies:
         copy.start()
-    away = [(group_slot[d] - group_slot[0] + 4) % 4 for d in (1, 2, 3)]
+    copies[0].wait()
+    away = [(slots[d] - slots[0] + 4) % 4 for d in (1, 2, 3)]
     index[0] = (away[0] - 1) * 2 + jnp.where(away[1] > away[2], 1, 0)
-    for copy in copies:
+    for copy in copies[1:]:
         copy.wait()
 
 
-def prepare(group_slot, tile_row, features):
+def prepare(features, group_slot, tile_row):
     return pl.pallas_call(
         prepare_kernel,
-        in_specs=[SMEM, SMEM, HBM],
+        in_specs=[HBM, HBM, SMEM],
         out_specs=[SMEM, VMEM],
         out_shape=[
             jax.ShapeDtypeStruct((1,), jnp.int32),
             jax.ShapeDtypeStruct((2, COLS, C), jnp.bfloat16),
         ],
-        scratch_shapes=[pltpu.SemaphoreType.DMA((2,))],
-    )(group_slot, tile_row, features)
+        scratch_shapes=[pltpu.SMEM((4,), jnp.int32), pltpu.SemaphoreType.DMA((3,))],
+    )(features, group_slot, tile_row)
 
 
 def cyclic_order(index):
@@ -317,7 +354,7 @@
     tile_row = (lax.axis_index("tile") // across).astype(jnp.int32).reshape(1)
     group = lax.axis_index("group").astype(jnp.int32).reshape(1)
     weights = kernel.reshape(3, DEPTH, C)
-    index, edge = prepare(group_slot, tile_row, features)
+    index, edge = prepare(features, group_slot, tile_row)
     conv_flops = 2 * 3 * CELLS * DEPTH * C
 
     def routed(order):
@@ -326,25 +363,27 @@
         def branch(features, edge, margins, tile_row, group_slot, group, gain, weights, bias):
             previous = lax.ppermute(features, "group", route)
             rim = lax.ppermute(edge, "tile", [(t, (t + across) % tiles) for t in range(tiles)])
-            stacked, columns, taps = call(
-                expand_kernel,
+            early, late, columns, taps = call(
+                expand_own_kernel,
                 (margins, features.reshape(2 * CELLS, C), gain, weights),
                 [SMEM, VMEM, VMEM, HBM],
                 [
-                    jax.ShapeDtypeStruct((2, CELLS, DEPTH), jnp.bfloat16),
+                    jax.ShapeDtypeStruct((CELLS, DEPTH), jnp.bfloat16),
+                    jax.ShapeDtypeStruct((CELLS, C), jnp.float32),
                     jax.ShapeDtypeStruct((2, 2, ROWS, C), jnp.bfloat16),
                     jax.ShapeDtypeStruct((DEPTH, 3 * C), jnp.bfloat16),
                 ],
                 [
                     COEFS,
                     SPARE,
+                    AHEAD,
                     pltpu.VMEM((2, 2, ROWS, C), jnp.float32),
+                    pltpu.VMEM((CELLS, DEPTH), jnp.bfloat16),
                     pltpu.SemaphoreType.DMA((3,)),
                 ],
-                2 * CELLS * DEPTH,
-                16,
-            )
-            own = call(own_kernel, (stacked, taps), [VMEM] * 2, PARTIAL, [], conv_flops, 16)
+                conv_flops // 3,
+                8,
+            )
             spare = jnp.zeros((2, COLS - ROWS - 1, C), jnp.bfloat16)
             first, last = (
                 jnp.concatenate([columns[side], rim[:, at : at + 1], spare], axis=1)
@@ -353,16 +392,22 @@
             inner = [t for t in range(tiles) if t % across != across - 1]
             left = lax.ppermute(last, "tile", [(t, t + 1) for t in inner])
             right = lax.ppermute(first, "tile", [(t + 1, t) for t in inner])
+            own = call(
+                own_kernel, (early, taps, late), [VMEM] * 3, PARTIAL, [], CELLS, 8
+            )
+            stacked = call(
+                expand_previous_kernel,
+                (margins, group_slot, group, previous.reshape(2 * CELLS, C), gain),
+                [SMEM, SMEM, SMEM, VMEM, VMEM],
+                jax.ShapeDtypeStruct((2, CELLS, DEPTH), jnp.bfloat16),
+                [COEFS, SPARE, AHEAD],
+                conv_flops // 3,
+                8,
+            )
             halo = jnp.stack([rim, left, right])
             halo_previous = lax.ppermute(halo, "group", route)
             sums = call(
-                previous_kernel,
-                (margins, group_slot, group, previous.reshape(2 * CELLS, C), gain, taps, own, bias),
-                [SMEM, SMEM, SMEM, VMEM, VMEM, VMEM, VMEM, VMEM],
-                PARTIAL,
-                [COEFS, SPARE, STACKED],
-                conv_flops,
-                16,
+                previous_kernel, (stacked, taps, own, bias), [VMEM] * 4, PARTIAL, [], conv_flops, 8
             )
             return call(
                 join_kernel,
@@ -377,7 +422,7 @@
                     pltpu.VMEM((3, 4 * 32, C), jnp.bfloat16),
                 ],
                 2 * 3 * 9 * 40 * C * C,
-                16,
+                8,
             )
 
         return branch

time: 41.6 us -> 40.3 us (0.969)
  Pallas kernels: 20.9 us -> 19.3 us
    pallas_call x4 -> x5, Pallas kernels: 19 us -> 18 us  [call(): pl.pallas_call(kernel, in_specs=specs, out_specs=[VMEM] * len(outputs) if...]
    pallas_call x1, Pallas kernels: 1.94 us -> 1.28 us  [prepare(): pl.pallas_call(prepare_kernel, in_specs=[HBM, HBM, SMEM], out_specs=[SMEM...]
  transfers between devices with their start and end apart: 5 -> 5, of which waited for: 0 -> 0; matrix products, arithmetic and copies ran while one was open for 0% -> 1% of each run, Pallas kernels for 39% -> 38%
where the time goes in v1:
time: 40.3 us; the launch traced here: 39.8 us
  Pallas kernels  19.3 us (48%)
  starting transfers between devices  18 us (45%)
  local copies, waits for them, and re-layouts  0.93 us (2%)
  loops' own time  0.71 us (2%)
  between operations  0.71 us (2%)
    pallas_call x5, Pallas kernels, call(): pl.pallas_call(kernel, in_specs=specs, out_specs=[VMEM] * len(outputs) if...  18 us
    ppermute x1, starting transfers between devices, branch(): lax.ppermute(edge, 'tile', [(t, (t + across) % tiles) for t in range(tile...  6.38 us
    ppermute x1, starting transfers between devices, branch(): right = lax.ppermute(first, 'tile', [(t + 1, t) for t in inner])  4.48 us
    ppermute x1, starting transfers between devices, branch(): left = lax.ppermute(last, 'tile', [(t, t + 1) for t in inner])  3.48 us
    ppermute x1, starting transfers between devices, branch(): previous = lax.ppermute(features, 'group', route)  2.76 us
    pallas_call x1, Pallas kernels, prepare(): pl.pallas_call(prepare_kernel, in_specs=[HBM, HBM, SMEM], out_specs=[SMEM...  1.28 us
    ppermute x1, starting transfers between devices, branch(): halo_previous = lax.ppermute(halo, 'group', route)  0.91 us
    unnamed x2, local copies, waits for them, and re-layouts  0.81 us
  transfers between devices with their start and end apart: 5, of which 0 were waited for; matrix products, arithmetic and copies ran while one was open for 1% of the time, Pallas kernels for 38%

profile of v1, /device:TPU:32, one launch (start us, length us, event | category | flops | bytes accessed | tf_op | source)
XLA Modules:
  0.0 39.8 jit_solution(3900476356416029922)
XLA Ops:
  0.0 1.3 %shard_map.94 = (s32[1]{0:T(128)}, bf16[2,24,384]{2,1,0:T(8,128)(2,1)S(1)}) custom-call(bf16[1,2,16,24,384]{4,3,2,1,0:T(8,128)(2,1)} %core.1, s32[4]{0:T(128)} %group_slot.1, s32[1]{0:T(128)} %bitcast.60.tile_row), custom_call_target="tpu_custom_call" | custom-call | tf_op jit(solution)/shard_map/pallas_call | solution.py:330
  2.0 37.0 %conditional.1 = (bf16[1,2,16,24,384]{4,3,2,1,0:T(8,128)(2,1)S(1)}) conditional(s32[]{:T(128)} %bitcast.61, (bf16[2,24,384]{2,1,0:T(8,128)(2,1)S(1)}, bf16[1,2,16,24,384]{4,3,2,1,0:T(8,128)(2,1)}, s32[1,4]{1,0:T(1,128)}, f32[384]{0:T(512)}, bf16[3,3,3,384,384]{4,3,2,1,0:T(8,128)(2,1)}, /*index=5*/s32[4]{0:T(128)}, ...), branch_computations={%region_0.1_spmd, %region_1.2_spmd, %region_2.3_spmd, %region_3.4_... | conditional | flops 5414898176 | bytes 8996160 | solution.py:430
  2.2 6.4 %collective-permute-start.25 = (bf16[2,24,384]{2,1,0:T(8,128)(2,1)S(1)}, bf16[2,24,384]{2,1,0:T(8,128)(2,1)S(1)}, u32[]{:S(2)}, u32[]{:S(2)}) collective-permute-start(bf16[2,24,384]{2,1,0:T(8,128)(2,1)S(1)} %get-tuple-element.190), channel_id=1, source_target_pairs={{0,32},{2,34},{4,36},{6,38},{8,40},{10,42},{12,44},{14,46},{16,48}... | collective-permute-start | bytes 110600 | tf_op jit(solution)/shard_map/cond/branch_5_fun/ppermute | solution.py:365
  8.6 2.8 %collective-permute-start.29 = (bf16[1,2,16,24,384]{4,3,2,1,0:T(8,128)(2,1)}, bf16[1,2,16,24,384]{4,3,2,1,0:T(8,128)(2,1)S(1)}, u32[]{:S(2)}, u32[]{:S(2)}) collective-permute-start(bf16[1,2,16,24,384]{4,3,2,1,0:T(8,128)(2,1)} %get-tuple-element.191), channel_id=1, source_target_pairs={{0,192},{192,128},{128,64},{64,0},{1,193},{193,129},{129,65},{65,1... | collective-permute-start | bytes 1769480 | tf_op jit(solution)/shard_map/cond/branch_5_fun/ppermute | solution.py:364
  11.4 5.4 %branch_5_fun.5 = (bf16[384,3456]{1,0:T(8,128)(2,1)S(1)}, f32[384,384]{1,0:T(8,128)S(1)}, bf16[2,2,16,384]{3,2,1,0:T(8,128)(2,1)S(1)}, bf16[3456,1152]{1,0:T(8,128)(2,1)S(1)}) custom-call(s32[1,4]{1,0:T(1,128)} %get-tuple-element.239.margins, bf16[768,384]{1,0:T(8,128)(2,1)} %bitcast.91, f32[384]{0:T(512)} %get-tuple-element.245.gain, ...), custom_call_target="tpu_custom_call" | custom-call | flops 1019215872 | bytes 995328 | tf_op jit(solution)/shard_map/cond/branch_5_fun/pallas_call | solution.py:302
  16.8 0.1 pad.53.clone
  16.8 0.0 collective-permute-done.25
  16.9 0.1 maximum_maximum_fusion.10
  17.0 3.5 %collective-permute-start.26 = (bf16[2,24,384]{2,1,0:T(8,128)(2,1)S(1)}, bf16[2,24,384]{2,1,0:T(8,128)(2,1)S(1)}, u32[]{:S(2)}, u32[]{:S(2)}) collective-permute-start(bf16[2,24,384]{2,1,0:T(8,128)(2,1)S(1)} %get-tuple-element.298), channel_id=1, source_target_pairs={{0,2},{2,4},{4,6},{6,8},{8,10},{10,12},{12,14},{14,16},{16,18},{18... | collective-permute-start | bytes 110600 | tf_op jit(solution)/shard_map/cond/branch_5_fun/ppermute | solution.py:393
  20.4 4.5 %collective-permute-start.27 = (bf16[2,24,384]{2,1,0:T(8,128)(2,1)S(1)}, bf16[2,24,384]{2,1,0:T(8,128)(2,1)S(1)}, u32[]{:S(2)}, u32[]{:S(2)}) collective-permute-start(bf16[2,24,384]{2,1,0:T(8,128)(2,1)S(1)} %get-tuple-element.299), channel_id=1, source_target_pairs={{2,0},{4,2},{6,4},{8,6},{10,8},{12,10},{14,12},{16,14},{18,16},{20... | collective-permute-start | bytes 110600 | tf_op jit(solution)/shard_map/cond/branch_5_fun/ppermute | solution.py:394
  24.9 0.0 copy-start.5
  24.9 0.0 copy-start.12
  24.9 0.0 copy-start.18
  25.0 3.5 %branch_5_fun.7.own = f32[2,384,384]{2,1,0:T(8,128)S(1)} custom-call(bf16[384,3456]{1,0:T(8,128)(2,1)S(1)} %get-tuple-element.196.early, bf16[3456,1152]{1,0:T(8,128)(2,1)S(1)} %get-tuple-element.195.taps, f32[384,384]{1,0:T(8,128)S(1)} %get-tuple-element.197.late), custom_call_target="tpu_custom_call" | custom-call | flops 384 | tf_op jit(solution)/shard_map/cond/branch_5_fun/pallas_call | solution.py:302
  28.5 0.0 collective-permute-done.26
  28.5 0.0 collective-permute-done.27
  28.5 0.9 %collective-permute-start.28 = (bf16[3,2,24,384]{3,2,1,0:T(8,128)(2,1)S(1)}, bf16[3,2,24,384]{3,2,1,0:T(8,128)(2,1)S(1)}, u32[]{:S(2)}, u32[]{:S(2)}) collective-permute-start(bf16[3,2,24,384]{3,2,1,0:T(8,128)(2,1)S(1)} %pad_maximum_fusion.5.halo), channel_id=1, source_target_pairs={{0,192},{192,128},{128,64},{64,0},{1,193},{193,129},{129,65},{65,1... | collective-permute-start | bytes 331784 | tf_op jit(solution)/shard_map/cond/branch_5_fun/ppermute | solution.py:408
  29.5 0.0 collective-permute-done.29
  29.5 0.0 copy-start.24
  29.5 2.2 %branch_5_fun.6.stacked = bf16[2,384,3456]{2,1,0:T(8,128)(2,1)S(1)} custom-call(s32[1,4]{1,0:T(1,128)S(1)} %copy-done.12, s32[4]{0:T(128)S(1)} %copy-done.18, s32[1]{0:T(128)} %bitcast.50.group, bf16[768,384]{1,0:T(8,128)(2,1)S(1)} %bitcast.79, f32[384]{0:T(512)S(1)} %copy-done.5), custom_call_target="tpu_custom_call" | custom-call | flops 1019215872 | bytes 995328 | tf_op jit(solution)/shard_map/cond/branch_5_fun/pallas_call | solution.py:302
  31.7 4.1 %branch_5_fun.8.sums = f32[2,384,384]{2,1,0:T(8,128)S(1)} custom-call(bf16[2,384,3456]{2,1,0:T(8,128)(2,1)S(1)} %branch_5_fun.6.stacked, bf16[3456,1152]{1,0:T(8,128)(2,1)S(1)} %get-tuple-element.195.taps, f32[2,384,384]{2,1,0:T(8,128)S(1)} %branch_5_fun.7.own, f32[384]{0:T(512)S(1)} %copy-done.24), custom_call_target="tpu_custom_call" | custom-call | flops 3057647616 | bytes 2985984 | tf_op jit(solution)/shard_map/cond/branch_5_fun/pallas_call | solution.py:302
  35.8 2.8 %branch_5_fun.9 = bf16[768,384]{1,0:T(8,128)(2,1)S(1)} custom-call(s32[1,4]{1,0:T(1,128)S(1)} %copy-done.12, s32[1]{0:T(128)} %get-tuple-element.187.tile_row, s32[4]{0:T(128)S(1)} %copy-done.18, s32[1]{0:T(128)} %bitcast.50.group, bf16[3,2,24,384]{3,2,1,0:T(8,128)(2,1)S(1)} %pad_maximum_fusion.5.halo, ...), custom_call_target="tpu_custom_call" | custom-call | flops 318504960 | bytes 311040 | tf_op jit(solution)/shard_map/cond/branch_5_fun/pallas_call | solution.py:302
  39.0 0.0 copy-start.6
  39.0 0.8 %copy-done.6 = bf16[1,2,16,24,384]{4,3,2,1,0:T(8,128)(2,1)} copy-done((bf16[1,2,16,24,384]{4,3,2,1,0:T(8,128)(2,1)}, bf16[1,2,16,24,384]{4,3,2,1,0:T(8,128)(2,1)S(1)}, u32[]{:S(2)}) %copy-start.6) | copy-done | bytes 589848
  (9 shorter events, 0.0 us)
Async XLA Ops:
  2.2 14.6 %collective-permute-start.25 = (bf16[2,24,384]{2,1,0:T(8,128)(2,1)S(1)}, bf16[2,24,384]{2,1,0:T(8,128)(2,1)S(1)}, u32[]{:S(2)}, u32[]{:S(2)}) collective-permute-start(bf16[2,24,384]{2,1,0:T(8,128)(2,1)S(1)} %get-tuple-element.190), channel_id=1, source_target_pairs={{0,32},{2,34},{4,36},{6,38},{8,40},{10,42},{12,44},{14,46},{16,48}... | collective-permute-start | bytes 110600 | tf_op jit(solution)/shard_map/cond/branch_5_fun/ppermute | solution.py:365
  8.6 20.8 %collective-permute-start.29 = (bf16[1,2,16,24,384]{4,3,2,1,0:T(8,128)(2,1)}, bf16[1,2,16,24,384]{4,3,2,1,0:T(8,128)(2,1)S(1)}, u32[]{:S(2)}, u32[]{:S(2)}) collective-permute-start(bf16[1,2,16,24,384]{4,3,2,1,0:T(8,128)(2,1)} %get-tuple-element.191), channel_id=1, source_target_pairs={{0,192},{192,128},{128,64},{64,0},{1,193},{193,129},{129,65},{65,1... | collective-permute-start | bytes 1769480 | tf_op jit(solution)/shard_map/cond/branch_5_fun/ppermute | solution.py:364
  17.0 11.5 %collective-permute-start.26 = (bf16[2,24,384]{2,1,0:T(8,128)(2,1)S(1)}, bf16[2,24,384]{2,1,0:T(8,128)(2,1)S(1)}, u32[]{:S(2)}, u32[]{:S(2)}) collective-permute-start(bf16[2,24,384]{2,1,0:T(8,128)(2,1)S(1)} %get-tuple-element.298), channel_id=1, source_target_pairs={{0,2},{2,4},{4,6},{6,8},{8,10},{10,12},{12,14},{14,16},{16,18},{18... | collective-permute-start | bytes 110600 | tf_op jit(solution)/shard_map/cond/branch_5_fun/ppermute | solution.py:393
  20.4 8.1 %collective-permute-start.27 = (bf16[2,24,384]{2,1,0:T(8,128)(2,1)S(1)}, bf16[2,24,384]{2,1,0:T(8,128)(2,1)S(1)}, u32[]{:S(2)}, u32[]{:S(2)}) collective-permute-start(bf16[2,24,384]{2,1,0:T(8,128)(2,1)S(1)} %get-tuple-element.299), channel_id=1, source_target_pairs={{2,0},{4,2},{6,4},{8,6},{10,8},{12,10},{14,12},{16,14},{18,16},{20... | collective-permute-start | bytes 110600 | tf_op jit(solution)/shard_map/cond/branch_5_fun/ppermute | solution.py:394
  24.9 4.5 %copy-start.5 = (f32[384]{0:T(512)S(1)}, f32[384]{0:T(512)}, u32[]{:S(2)}) copy-start(f32[384]{0:T(512)} %get-tuple-element.245.gain) | copy-start | bytes 4612 | tf_op jit(solution)/shard_map/cond
  24.9 4.5 %copy-start.12 = (s32[1,4]{1,0:T(1,128)S(1)}, s32[1,4]{1,0:T(1,128)}, u32[]{:S(2)}) copy-start(s32[1,4]{1,0:T(1,128)} %get-tuple-element.239.margins) | copy-start | bytes 52 | tf_op jit(solution)/shard_map/cond
  24.9 4.5 %copy-start.18 = (s32[4]{0:T(128)S(1)}, s32[4]{0:T(128)}, u32[]{:S(2)}) copy-start(s32[4]{0:T(128)} %get-tuple-element.188.group_slot) | copy-start | bytes 52 | tf_op jit(solution)/shard_map/cond
  28.5 7.3 %collective-permute-start.28 = (bf16[3,2,24,384]{3,2,1,0:T(8,128)(2,1)S(1)}, bf16[3,2,24,384]{3,2,1,0:T(8,128)(2,1)S(1)}, u32[]{:S(2)}, u32[]{:S(2)}) collective-permute-start(bf16[3,2,24,384]{3,2,1,0:T(8,128)(2,1)S(1)} %pad_maximum_fusion.5.halo), channel_id=1, source_target_pairs={{0,192},{192,128},{128,64},{64,0},{1,193},{193,129},{129,65},{65,1... | collective-permute-start | bytes 331784 | tf_op jit(solution)/shard_map/cond/branch_5_fun/ppermute | solution.py:408
  29.5 2.2 %copy-start.24 = (f32[384]{0:T(512)S(1)}, f32[384]{0:T(512)}, u32[]{:S(2)}) copy-start(f32[384]{0:T(512)} %get-tuple-element.257.bias) | copy-start | bytes 4612 | tf_op jit(solution)/shard_map/cond
  39.0 0.8 %copy-start.6 = (bf16[1,2,16,24,384]{4,3,2,1,0:T(8,128)(2,1)}, bf16[1,2,16,24,384]{4,3,2,1,0:T(8,128)(2,1)S(1)}, u32[]{:S(2)}) copy-start(bf16[1,2,16,24,384]{4,3,2,1,0:T(8,128)(2,1)S(1)} %get-tuple-element.330) | copy-start | bytes 1769476

commit v2 on v1

--- a/solution.py
+++ b/solution.py
@@ -103,17 +103,21 @@
             put(f, ROWS // 2 - 1, 2, e, [spare[f, e], jnp.zeros((COLS, C), jnp.float32)], False)
 
 
+def across(coef):
+    return jnp.concatenate([coef] * (C // 128), axis=1)
+
+
 def fill_row_coefs(margins, row_coefs):
-    row = lax.broadcasted_iota(jnp.int32, (ROWS, C), 0)
+    row = lax.broadcasted_iota(jnp.int32, (ROWS, 128), 0)
     for n, b in enumerate((0, 2)):
-        row_coefs[n] = blend_coef(row, b, ROWS, margins[0, 2], margins[0, 3])
+        row_coefs[n] = across(blend_coef(row, b, ROWS, margins[0, 2], margins[0, 3]))
 
 
 def column_coefs(margins):
-    place = lax.broadcasted_iota(jnp.int32, (8, C), 0)
+    place = lax.broadcasted_iota(jnp.int32, (8, 128), 0)
     coef_first = blend_coef(place + (COLS - 8), 0, COLS, margins[0, 0], margins[0, 1])
     coef_last = blend_coef(place, 2, COLS, margins[0, 0], margins[0, 1])
-    return coef_first, coef_last
+    return across(coef_first), across(coef_last)
 
 
 def dot(a, b):
@@ -212,11 +216,9 @@
     halo_previous,
     gain,
     taps,
-    sums,
-    out,
-    row_coefs,
     sides,
     near,
+    row_coefs,
     columns,
     rims,
 ):
@@ -238,16 +240,17 @@
             at = 2 * n + f
             for e in range(3):
                 values = jnp.concatenate([views[e], jnp.zeros((8, C), jnp.float32)], axis=0)
-                rims[e, pl.ds(pl.multiple_of(at * 32, 32), 32), :] = values.astype(jnp.bfloat16)
+                rims[e, at * 32 : at * 32 + 32, :] = values.astype(jnp.bfloat16)
             for side, column in enumerate((left[:ROWS], right[:ROWS])):
                 above = jnp.concatenate([none, column[: ROWS - 1]], axis=0) * row_coefs[0]
                 below = jnp.concatenate([column[1:], none], axis=0) * row_coefs[1]
                 for b, values in enumerate((above, column, below)):
-                    rows = pl.ds(pl.multiple_of(at * ROWS, 16), ROWS)
+                    rows = slice(at * ROWS, (at + 1) * ROWS)
                     columns[3 * side + b, rows, :] = values.astype(jnp.bfloat16)
         return 0
 
-    lax.fori_loop(0, 2, frames, 0)
+    for f in range(2):
+        frames(f, 0)
     sides[...] = jnp.zeros_like(sides)
     near[...] = jnp.zeros_like(near)
     first = jnp.where(top, 0, 6)
@@ -268,26 +271,31 @@
         return 0
 
     lax.fori_loop(0, 3, times, 0)
+
+
+def finish_kernel(tile_row, sums, sides, near, out):
+    top = tile_row[0] == 1
     place = lax.broadcasted_iota(jnp.int32, (8, C), 0)
-
-    def two_rows(k, _):
-        for f in range(2):
-            block = sums[f, pl.ds(pl.multiple_of(k * PAIR, 16), PAIR), :]
-            beside = near[32 * f : 32 * f + COLS]
+    for f in range(2):
+        beside = near[32 * f : 32 * f + COLS]
+        for k in range(ROWS // 2):
+            block = sums[f, k * PAIR : (k + 1) * PAIR]
             parts = []
-            for n, here in enumerate((top & (k == 0), ~top & (k == ROWS // 2 - 1))):
-                values = block[n * COLS : (n + 1) * COLS] + jnp.where(here, beside, 0.0)
-                at = pl.ds(f * ROWS + 2 * k + n, 1)
+            for n in range(2):
+                row = 2 * k + n
+                values = block[n * COLS : (n + 1) * COLS]
+                if row == 0:
+                    values = values + jnp.where(top, beside, 0.0)
+                if row == ROWS - 1:
+                    values = values + jnp.where(top, 0.0, beside)
+                at = slice(f * ROWS + row, f * ROWS + row + 1)
                 parts += [
-                    values[:8] + jnp.where(place == 0, sides[0, at, :], 0.0),
+                    values[:8] + jnp.where(place == 0, sides[0, at], 0.0),
                     values[8:16],
-                    values[16:] + jnp.where(place == 7, sides[1, at, :], 0.0),
+                    values[16:] + jnp.where(place == 7, sides[1, at], 0.0),
                 ]
-            rows = pl.ds(pl.multiple_of(f * CELLS + k * PAIR, 16), PAIR)
-            out[rows, :] = jnp.concatenate(parts, axis=0).astype(jnp.bfloat16)
-        return 0
-
-    lax.fori_loop(0, ROWS // 2, two_rows, 0)
+            rows = slice(f * CELLS + k * PAIR, f * CELLS + (k + 1) * PAIR)
+            out[rows] = jnp.concatenate(parts, axis=0).astype(jnp.bfloat16)
 
 
 SMEM, VMEM, HBM = (pl.BlockSpec(memory_space=m) for m in (pltpu.SMEM, pltpu.VMEM, pl.ANY))
@@ -405,29 +413,33 @@
                 8,
             )
             halo = jnp.stack([rim, left, right])
+            halo, own = lax.optimization_barrier((halo, own))
             halo_previous = lax.ppermute(halo, "group", route)
             sums = call(
                 previous_kernel, (stacked, taps, own, bias), [VMEM] * 4, PARTIAL, [], conv_flops, 8
             )
-            return call(
+            halo_previous, sums = lax.optimization_barrier((halo_previous, sums))
+            sides, near = call(
                 join_kernel,
-                (margins, tile_row, group_slot, group, halo, halo_previous, gain, taps, sums),
-                [SMEM] * 4 + [VMEM] * 5,
-                jax.ShapeDtypeStruct((2 * CELLS, C), jnp.bfloat16),
+                (margins, tile_row, group_slot, group, halo, halo_previous, gain, taps),
+                [SMEM] * 4 + [VMEM] * 4,
+                [
+                    jax.ShapeDtypeStruct((2, 2 * ROWS, C), jnp.float32),
+                    jax.ShapeDtypeStruct((64, C), jnp.float32),
+                ],
                 [
                     COEFS,
-                    pltpu.VMEM((2, 2 * ROWS, C), jnp.float32),
-                    pltpu.VMEM((64, C), jnp.float32),
                     pltpu.VMEM((6, 4 * ROWS, C), jnp.bfloat16),
                     pltpu.VMEM((3, 4 * 32, C), jnp.bfloat16),
                 ],
                 2 * 3 * 9 * 40 * C * C,
                 8,
             )
+            return sums, sides, near
 
         return branch
 
-    decoded = lax.switch(
+    sums, sides, near = lax.switch(
         index[0],
         [routed(cyclic_order(n)) for n in range(6)],
         features,
@@ -439,6 +451,15 @@
         norm_gain,
         weights,
         conv_bias,
+    )
+    decoded = call(
+        finish_kernel,
+        (tile_row, sums, sides, near),
+        [SMEM, VMEM, VMEM, VMEM],
+        jax.ShapeDtypeStruct((2 * CELLS, C), jnp.bfloat16),
+        [],
+        2 * CELLS * C,
+        8,
     )
     return decoded.reshape(1, 2, ROWS, COLS, C)
 

time: 40.3 us -> 40.2 us (level); the launches traced: 39.8 us -> 40.1 us
  local copies, waits for them, and re-layouts: 0.93 us -> 0.12 us
  starting transfers between devices: 18 us -> 18.6 us
  Pallas kernels: 19.3 us -> 19.9 us
    unnamed x2 -> x0, local copies, waits for them, and re-layouts: 0.81 us -> none
    pallas_call x5 -> x6, Pallas kernels: 18 us -> 18.6 us  [call(): pl.pallas_call(kernel, in_specs=specs, out_specs=[VMEM] * len(outputs) if...]
    ppermute x1, starting transfers between devices: 0.91 us -> 1.5 us  [branch(): halo_previous = lax.ppermute(halo, 'group', route)]
where the time goes in v2:
time: 40.2 us; the launch traced here: 40.1 us
  Pallas kernels  19.9 us (50%)
  starting transfers between devices  18.6 us (46%)
  loops' own time  0.71 us (2%)
  between operations  0.67 us (2%)
    pallas_call x6, Pallas kernels, call(): pl.pallas_call(kernel, in_specs=specs, out_specs=[VMEM] * len(outputs) if...  18.6 us
    ppermute x1, starting transfers between devices, branch(): lax.ppermute(edge, 'tile', [(t, (t + across) % tiles) for t in range(tile...  6.38 us
    ppermute x1, starting transfers between devices, branch(): right = lax.ppermute(first, 'tile', [(t + 1, t) for t in inner])  4.47 us
    ppermute x1, starting transfers between devices, branch(): left = lax.ppermute(last, 'tile', [(t, t + 1) for t in inner])  3.48 us
    ppermute x1, starting transfers between devices, branch(): previous = lax.ppermute(features, 'group', route)  2.76 us
    ppermute x1, starting transfers between devices, branch(): halo_previous = lax.ppermute(halo, 'group', route)  1.5 us
    pallas_call x1, Pallas kernels, prepare(): pl.pallas_call(prepare_kernel, in_specs=[HBM, HBM, SMEM], out_specs=[SMEM...  1.28 us
  transfers between devices with their start and end apart: 5, of which 0 were waited for; matrix products, arithmetic and copies ran while one was open for 1% of the time, Pallas kernels for 38%

profile of v2, /device:TPU:32, one launch (start us, length us, event | category | flops | bytes accessed | tf_op | source)
XLA Modules:
  0.0 40.1 jit_solution(5337286425642809796)
XLA Ops:
  0.0 1.3 %shard_map.64 = (s32[1]{0:T(128)}, bf16[2,24,384]{2,1,0:T(8,128)(2,1)S(1)}) custom-call(bf16[1,2,16,24,384]{4,3,2,1,0:T(8,128)(2,1)} %core.1, s32[4]{0:T(128)} %group_slot.1, s32[1]{0:T(128)} %bitcast.42.tile_row), custom_call_target="tpu_custom_call" | custom-call | tf_op jit(solution)/shard_map/pallas_call | solution.py:338
  1.9 37.2 %conditional.1 = (f32[2,384,384]{2,1,0:T(8,128)S(1)}, f32[2,32,384]{2,1,0:T(8,128)S(1)}, f32[64,384]{1,0:T(8,128)S(1)}) conditional(s32[]{:T(128)} %bitcast.43, (bf16[2,24,384]{2,1,0:T(8,128)(2,1)S(1)}, bf16[1,2,16,24,384]{4,3,2,1,0:T(8,128)(2,1)}, s32[1,4]{1,0:T(1,128)}, f32[384]{0:T(512)}, ...), branch_computations={%region_0.1_spmd, %region_1.2_spmd, %region_2.3_spmd, %region_3.4_... | conditional | flops 5414898176 | bytes 8996176 | solution.py:442
  2.2 6.4 %collective-permute-start.15 = (bf16[2,24,384]{2,1,0:T(8,128)(2,1)S(1)}, bf16[2,24,384]{2,1,0:T(8,128)(2,1)S(1)}, u32[]{:S(2)}, u32[]{:S(2)}) collective-permute-start(bf16[2,24,384]{2,1,0:T(8,128)(2,1)S(1)} %get-tuple-element.170), channel_id=1, source_target_pairs={{0,32},{2,34},{4,36},{6,38},{8,40},{10,42},{12,44},{14,46},{16,48}... | collective-permute-start | bytes 110600 | tf_op jit(solution)/shard_map/cond/branch_3_fun/ppermute | solution.py:373
  8.6 2.8 %collective-permute-start.19 = (bf16[1,2,16,24,384]{4,3,2,1,0:T(8,128)(2,1)}, bf16[1,2,16,24,384]{4,3,2,1,0:T(8,128)(2,1)S(1)}, u32[]{:S(2)}, u32[]{:S(2)}) collective-permute-start(bf16[1,2,16,24,384]{4,3,2,1,0:T(8,128)(2,1)} %get-tuple-element.172), channel_id=1, source_target_pairs={{0,192},{192,64},{64,128},{128,0},{1,193},{193,65},{65,129},{129,1... | collective-permute-start | bytes 1769480 | tf_op jit(solution)/shard_map/cond/branch_3_fun/ppermute | solution.py:372
  11.3 5.4 %branch_3_fun.5 = (bf16[384,3456]{1,0:T(8,128)(2,1)S(1)}, f32[384,384]{1,0:T(8,128)S(1)}, bf16[2,2,16,384]{3,2,1,0:T(8,128)(2,1)S(1)}, bf16[3456,1152]{1,0:T(8,128)(2,1)S(1)}) custom-call(s32[1,4]{1,0:T(1,128)} %get-tuple-element.171.margins, bf16[768,384]{1,0:T(8,128)(2,1)} %bitcast.74, f32[384]{0:T(512)} %get-tuple-element.173.gain, ...), custom_call_target="tpu_custom_call" | custom-call | flops 1019215872 | bytes 995328 | tf_op jit(solution)/shard_map/cond/branch_3_fun/pallas_call | solution.py:310
  16.7 0.1 pad.35.clone
  16.8 0.0 collective-permute-done.15
  16.8 0.1 maximum_maximum_fusion.6
  16.9 3.5 %collective-permute-start.16 = (bf16[2,24,384]{2,1,0:T(8,128)(2,1)S(1)}, bf16[2,24,384]{2,1,0:T(8,128)(2,1)S(1)}, u32[]{:S(2)}, u32[]{:S(2)}) collective-permute-start(bf16[2,24,384]{2,1,0:T(8,128)(2,1)S(1)} %get-tuple-element.259), channel_id=1, source_target_pairs={{0,2},{2,4},{4,6},{6,8},{8,10},{10,12},{12,14},{14,16},{16,18},{18... | collective-permute-start | bytes 110600 | tf_op jit(solution)/shard_map/cond/branch_3_fun/ppermute | solution.py:401
  20.4 4.5 %collective-permute-start.17 = (bf16[2,24,384]{2,1,0:T(8,128)(2,1)S(1)}, bf16[2,24,384]{2,1,0:T(8,128)(2,1)S(1)}, u32[]{:S(2)}, u32[]{:S(2)}) collective-permute-start(bf16[2,24,384]{2,1,0:T(8,128)(2,1)S(1)} %get-tuple-element.260), channel_id=1, source_target_pairs={{2,0},{4,2},{6,4},{8,6},{10,8},{12,10},{14,12},{16,14},{18,16},{20... | collective-permute-start | bytes 110600 | tf_op jit(solution)/shard_map/cond/branch_3_fun/ppermute | solution.py:402
  24.9 0.0 copy-start.3
  24.9 0.0 copy-start.9
  24.9 0.0 copy-start.15
  24.9 3.5 %branch_3_fun.6.own = f32[2,384,384]{2,1,0:T(8,128)S(1)} custom-call(bf16[384,3456]{1,0:T(8,128)(2,1)S(1)} %get-tuple-element.176.early, bf16[3456,1152]{1,0:T(8,128)(2,1)S(1)} %get-tuple-element.177.taps, f32[384,384]{1,0:T(8,128)S(1)} %get-tuple-element.178.late), custom_call_target="tpu_custom_call" | custom-call | flops 384 | tf_op jit(solution)/shard_map/cond/branch_3_fun/pallas_call | solution.py:310
  28.4 0.0 collective-permute-done.16
  28.4 0.0 collective-permute-done.17
  28.5 1.5 %collective-permute-start.18 = (bf16[3,2,24,384]{3,2,1,0:T(8,128)(2,1)S(1)}, bf16[3,2,24,384]{3,2,1,0:T(8,128)(2,1)S(1)}, u32[]{:S(2)}, u32[]{:S(2)}) collective-permute-start(bf16[3,2,24,384]{3,2,1,0:T(8,128)(2,1)S(1)} %pad_maximum_fusion.3.halo), channel_id=1, source_target_pairs={{0,192},{192,64},{64,128},{128,0},{1,193},{193,65},{65,129},{129,1... | collective-permute-start | bytes 331784 | tf_op jit(solution)/shard_map/cond/branch_3_fun/ppermute | solution.py:417
  30.0 0.0 collective-permute-done.19
  30.0 0.0 copy-start.21
  30.0 2.2 %branch_3_fun.7.stacked = bf16[2,384,3456]{2,1,0:T(8,128)(2,1)S(1)} custom-call(s32[1,4]{1,0:T(1,128)S(1)} %copy-done.9, s32[4]{0:T(128)S(1)} %copy-done.15, s32[1]{0:T(128)} %get-tuple-element.181.group, bf16[768,384]{1,0:T(8,128)(2,1)S(1)} %bitcast.62, f32[384]{0:T(512)S(1)} %copy-done.3), custom_call_target="tpu_custom_call" | custom-call | flops 1019215872 | bytes 995328 | tf_op jit(solution)/shard_map/cond/branch_3_fun/pallas_call | solution.py:310
  32.3 4.1 %branch_3_fun.8 = f32[2,384,384]{2,1,0:T(8,128)S(1)} custom-call(bf16[2,384,3456]{2,1,0:T(8,128)(2,1)S(1)} %branch_3_fun.7.stacked, bf16[3456,1152]{1,0:T(8,128)(2,1)S(1)} %get-tuple-element.177.taps, f32[2,384,384]{2,1,0:T(8,128)S(1)} %branch_3_fun.6.own, f32[384]{0:T(512)S(1)} %copy-done.21), custom_call_target="tpu_custom_call" | custom-call | flops 3057647616 | bytes 2985984 | tf_op jit(solution)/shard_map/cond/branch_3_fun/pallas_call | solution.py:310
  36.4 0.0 collective-permute-done.18.halo_previous
  36.4 2.5 %branch_3_fun.9 = (f32[2,32,384]{2,1,0:T(8,128)S(1)}, f32[64,384]{1,0:T(8,128)S(1)}) custom-call(s32[1,4]{1,0:T(1,128)S(1)} %copy-done.9, s32[1]{0:T(128)} %get-tuple-element.185.tile_row, s32[4]{0:T(128)S(1)} %copy-done.15, s32[1]{0:T(128)} %get-tuple-element.181.group, bf16[3,2,24,384]{3,2,1,0:T(8,128)(2,1)S(1)} %pad_maximum_fusion.3.halo, ...), custom_call_target="tpu_custom_call" | custom-call | flops 318504960 | bytes 311040 | tf_op jit(solution)/shard_map/cond/branch_3_fun/pallas_call | solution.py:310
  39.1 1.0 %shard_map.65 = bf16[768,384]{1,0:T(8,128)(2,1)} custom-call(s32[1]{0:T(128)} %bitcast.42.tile_row, f32[2,384,384]{2,1,0:T(8,128)S(1)} %get-tuple-element.234.sums, f32[2,32,384]{2,1,0:T(8,128)S(1)} %get-tuple-element.235.sides, f32[64,384]{1,0:T(8,128)S(1)} %get-tuple-element.236.near), custom_call_target="tpu_custom_call" | custom-call | flops 294912 | bytes 288 | tf_op jit(solution)/shard_map/pallas_call | solution.py:310
  (8 shorter events, 0.0 us)
Async XLA Ops:
  2.2 14.6 %collective-permute-start.15 = (bf16[2,24,384]{2,1,0:T(8,128)(2,1)S(1)}, bf16[2,24,384]{2,1,0:T(8,128)(2,1)S(1)}, u32[]{:S(2)}, u32[]{:S(2)}) collective-permute-start(bf16[2,24,384]{2,1,0:T(8,128)(2,1)S(1)} %get-tuple-element.170), channel_id=1, source_target_pairs={{0,32},{2,34},{4,36},{6,38},{8,40},{10,42},{12,44},{14,46},{16,48}... | collective-permute-start | bytes 110600 | tf_op jit(solution)/shard_map/cond/branch_3_fun/ppermute | solution.py:373
  8.6 21.4 %collective-permute-start.19 = (bf16[1,2,16,24,384]{4,3,2,1,0:T(8,128)(2,1)}, bf16[1,2,16,24,384]{4,3,2,1,0:T(8,128)(2,1)S(1)}, u32[]{:S(2)}, u32[]{:S(2)}) collective-permute-start(bf16[1,2,16,24,384]{4,3,2,1,0:T(8,128)(2,1)} %get-tuple-element.172), channel_id=1, source_target_pairs={{0,192},{192,64},{64,128},{128,0},{1,193},{193,65},{65,129},{129,1... | collective-permute-start | bytes 1769480 | tf_op jit(solution)/shard_map/cond/branch_3_fun/ppermute | solution.py:372
  16.9 11.5 %collective-permute-start.16 = (bf16[2,24,384]{2,1,0:T(8,128)(2,1)S(1)}, bf16[2,24,384]{2,1,0:T(8,128)(2,1)S(1)}, u32[]{:S(2)}, u32[]{:S(2)}) collective-permute-start(bf16[2,24,384]{2,1,0:T(8,128)(2,1)S(1)} %get-tuple-element.259), channel_id=1, source_target_pairs={{0,2},{2,4},{4,6},{6,8},{8,10},{10,12},{12,14},{14,16},{16,18},{18... | collective-permute-start | bytes 110600 | tf_op jit(solution)/shard_map/cond/branch_3_fun/ppermute | solution.py:401
  20.4 8.1 %collective-permute-start.17 = (bf16[2,24,384]{2,1,0:T(8,128)(2,1)S(1)}, bf16[2,24,384]{2,1,0:T(8,128)(2,1)S(1)}, u32[]{:S(2)}, u32[]{:S(2)}) collective-permute-start(bf16[2,24,384]{2,1,0:T(8,128)(2,1)S(1)} %get-tuple-element.260), channel_id=1, source_target_pairs={{2,0},{4,2},{6,4},{8,6},{10,8},{12,10},{14,12},{16,14},{18,16},{20... | collective-permute-start | bytes 110600 | tf_op jit(solution)/shard_map/cond/branch_3_fun/ppermute | solution.py:402
  24.9 5.1 %copy-start.3 = (f32[384]{0:T(512)S(1)}, f32[384]{0:T(512)}, u32[]{:S(2)}) copy-start(f32[384]{0:T(512)} %get-tuple-element.173.gain) | copy-start | bytes 4612 | tf_op jit(solution)/shard_map/cond
  24.9 5.1 %copy-start.9 = (s32[1,4]{1,0:T(1,128)S(1)}, s32[1,4]{1,0:T(1,128)}, u32[]{:S(2)}) copy-start(s32[1,4]{1,0:T(1,128)} %get-tuple-element.171.margins) | copy-start | bytes 52 | tf_op jit(solution)/shard_map/cond
  24.9 5.1 %copy-start.15 = (s32[4]{0:T(128)S(1)}, s32[4]{0:T(128)}, u32[]{:S(2)}) copy-start(s32[4]{0:T(128)} %get-tuple-element.180.group_slot) | copy-start | bytes 52 | tf_op jit(solution)/shard_map/cond
  28.5 7.9 %collective-permute-start.18 = (bf16[3,2,24,384]{3,2,1,0:T(8,128)(2,1)S(1)}, bf16[3,2,24,384]{3,2,1,0:T(8,128)(2,1)S(1)}, u32[]{:S(2)}, u32[]{:S(2)}) collective-permute-start(bf16[3,2,24,384]{3,2,1,0:T(8,128)(2,1)S(1)} %pad_maximum_fusion.3.halo), channel_id=1, source_target_pairs={{0,192},{192,64},{64,128},{128,0},{1,193},{193,65},{65,129},{129,1... | collective-permute-start | bytes 331784 | tf_op jit(solution)/shard_map/cond/branch_3_fun/ppermute | solution.py:417
  30.0 2.2 %copy-start.21 = (f32[384]{0:T(512)S(1)}, f32[384]{0:T(512)}, u32[]{:S(2)}) copy-start(f32[384]{0:T(512)} %get-tuple-element.183.bias) | copy-start | bytes 4612 | tf_op jit(solution)/shard_map/cond

commit v3 on v1

--- a/solution.py
+++ b/solution.py
@@ -103,17 +103,21 @@
             put(f, ROWS // 2 - 1, 2, e, [spare[f, e], jnp.zeros((COLS, C), jnp.float32)], False)
 
 
+def across(coef):
+    return jnp.concatenate([coef] * (C // 128), axis=1)
+
+
 def fill_row_coefs(margins, row_coefs):
-    row = lax.broadcasted_iota(jnp.int32, (ROWS, C), 0)
+    row = lax.broadcasted_iota(jnp.int32, (ROWS, 128), 0)
     for n, b in enumerate((0, 2)):
-        row_coefs[n] = blend_coef(row, b, ROWS, margins[0, 2], margins[0, 3])
+        row_coefs[n] = across(blend_coef(row, b, ROWS, margins[0, 2], margins[0, 3]))
 
 
 def column_coefs(margins):
-    place = lax.broadcasted_iota(jnp.int32, (8, C), 0)
+    place = lax.broadcasted_iota(jnp.int32, (8, 128), 0)
     coef_first = blend_coef(place + (COLS - 8), 0, COLS, margins[0, 0], margins[0, 1])
     coef_last = blend_coef(place, 2, COLS, margins[0, 0], margins[0, 1])
-    return coef_first, coef_last
+    return across(coef_first), across(coef_last)
 
 
 def dot(a, b):

time: 40.3 us -> 40 us (level)
  no operation moved by 1% of the time
where the time goes in v3:
time: 40 us; the launch traced here: 39.8 us
  Pallas kernels  19.3 us (48%)
  starting transfers between devices  18 us (45%)
  local copies, waits for them, and re-layouts  0.93 us (2%)
  loops' own time  0.71 us (2%)
  between operations  0.71 us (2%)
    pallas_call x5, Pallas kernels, call(): pl.pallas_call(kernel, in_specs=specs, out_specs=[VMEM] * len(outputs) if...  18 us
    ppermute x1, starting transfers between devices, branch(): lax.ppermute(edge, 'tile', [(t, (t + across) % tiles) for t in range(tile...  6.38 us
    ppermute x1, starting transfers between devices, branch(): right = lax.ppermute(first, 'tile', [(t + 1, t) for t in inner])  4.48 us
    ppermute x1, starting transfers between devices, branch(): left = lax.ppermute(last, 'tile', [(t, t + 1) for t in inner])  3.48 us
    ppermute x1, starting transfers between devices, branch(): previous = lax.ppermute(features, 'group', route)  2.76 us
    pallas_call x1, Pallas kernels, prepare(): pl.pallas_call(prepare_kernel, in_specs=[HBM, HBM, SMEM], out_specs=[SMEM...  1.28 us
    ppermute x1, starting transfers between devices, branch(): halo_previous = lax.ppermute(halo, 'group', route)  0.91 us
    unnamed x2, local copies, waits for them, and re-layouts  0.81 us
  transfers between devices with their start and end apart: 5, of which 0 were waited for; matrix products, arithmetic and copies ran while one was open for 1% of the time, Pallas kernels for 38%

profile of v3, /device:TPU:32, one launch (start us, length us, event | category | flops | bytes accessed | tf_op | source)
XLA Modules:
  0.0 39.8 jit_solution(3900476356416029922)
XLA Ops:
  0.0 1.3 %shard_map.94 = (s32[1]{0:T(128)}, bf16[2,24,384]{2,1,0:T(8,128)(2,1)S(1)}) custom-call(bf16[1,2,16,24,384]{4,3,2,1,0:T(8,128)(2,1)} %core.1, s32[4]{0:T(128)} %group_slot.1, s32[1]{0:T(128)} %bitcast.60.tile_row), custom_call_target="tpu_custom_call" | custom-call | tf_op jit(solution)/shard_map/pallas_call | solution.py:334
  2.0 37.0 %conditional.1 = (bf16[1,2,16,24,384]{4,3,2,1,0:T(8,128)(2,1)S(1)}) conditional(s32[]{:T(128)} %bitcast.61, (bf16[2,24,384]{2,1,0:T(8,128)(2,1)S(1)}, bf16[1,2,16,24,384]{4,3,2,1,0:T(8,128)(2,1)}, s32[1,4]{1,0:T(1,128)}, f32[384]{0:T(512)}, bf16[3,3,3,384,384]{4,3,2,1,0:T(8,128)(2,1)}, /*index=5*/s32[4]{0:T(128)}, ...), branch_computations={%region_0.1_spmd, %region_1.2_spmd, %region_2.3_spmd, %region_3.4_... | conditional | flops 5414898176 | bytes 8996160 | solution.py:434
  2.2 6.4 %collective-permute-start.25 = (bf16[2,24,384]{2,1,0:T(8,128)(2,1)S(1)}, bf16[2,24,384]{2,1,0:T(8,128)(2,1)S(1)}, u32[]{:S(2)}, u32[]{:S(2)}) collective-permute-start(bf16[2,24,384]{2,1,0:T(8,128)(2,1)S(1)} %get-tuple-element.190), channel_id=1, source_target_pairs={{0,32},{2,34},{4,36},{6,38},{8,40},{10,42},{12,44},{14,46},{16,48}... | collective-permute-start | bytes 110600 | tf_op jit(solution)/shard_map/cond/branch_5_fun/ppermute | solution.py:369
  8.6 2.8 %collective-permute-start.29 = (bf16[1,2,16,24,384]{4,3,2,1,0:T(8,128)(2,1)}, bf16[1,2,16,24,384]{4,3,2,1,0:T(8,128)(2,1)S(1)}, u32[]{:S(2)}, u32[]{:S(2)}) collective-permute-start(bf16[1,2,16,24,384]{4,3,2,1,0:T(8,128)(2,1)} %get-tuple-element.191), channel_id=1, source_target_pairs={{0,192},{192,128},{128,64},{64,0},{1,193},{193,129},{129,65},{65,1... | collective-permute-start | bytes 1769480 | tf_op jit(solution)/shard_map/cond/branch_5_fun/ppermute | solution.py:368
  11.4 5.4 %branch_5_fun.5 = (bf16[384,3456]{1,0:T(8,128)(2,1)S(1)}, f32[384,384]{1,0:T(8,128)S(1)}, bf16[2,2,16,384]{3,2,1,0:T(8,128)(2,1)S(1)}, bf16[3456,1152]{1,0:T(8,128)(2,1)S(1)}) custom-call(s32[1,4]{1,0:T(1,128)} %get-tuple-element.239.margins, bf16[768,384]{1,0:T(8,128)(2,1)} %bitcast.91, f32[384]{0:T(512)} %get-tuple-element.245.gain, ...), custom_call_target="tpu_custom_call" | custom-call | flops 1019215872 | bytes 995328 | tf_op jit(solution)/shard_map/cond/branch_5_fun/pallas_call | solution.py:306
  16.8 0.1 pad.53.clone
  16.8 0.0 collective-permute-done.25
  16.9 0.1 maximum_maximum_fusion.10
  17.0 3.5 %collective-permute-start.26 = (bf16[2,24,384]{2,1,0:T(8,128)(2,1)S(1)}, bf16[2,24,384]{2,1,0:T(8,128)(2,1)S(1)}, u32[]{:S(2)}, u32[]{:S(2)}) collective-permute-start(bf16[2,24,384]{2,1,0:T(8,128)(2,1)S(1)} %get-tuple-element.298), channel_id=1, source_target_pairs={{0,2},{2,4},{4,6},{6,8},{8,10},{10,12},{12,14},{14,16},{16,18},{18... | collective-permute-start | bytes 110600 | tf_op jit(solution)/shard_map/cond/branch_5_fun/ppermute | solution.py:397
  20.4 4.5 %collective-permute-start.27 = (bf16[2,24,384]{2,1,0:T(8,128)(2,1)S(1)}, bf16[2,24,384]{2,1,0:T(8,128)(2,1)S(1)}, u32[]{:S(2)}, u32[]{:S(2)}) collective-permute-start(bf16[2,24,384]{2,1,0:T(8,128)(2,1)S(1)} %get-tuple-element.299), channel_id=1, source_target_pairs={{2,0},{4,2},{6,4},{8,6},{10,8},{12,10},{14,12},{16,14},{18,16},{20... | collective-permute-start | bytes 110600 | tf_op jit(solution)/shard_map/cond/branch_5_fun/ppermute | solution.py:398
  24.9 0.0 copy-start.5
  24.9 0.0 copy-start.12
  24.9 0.0 copy-start.18
  25.0 3.5 %branch_5_fun.7.own = f32[2,384,384]{2,1,0:T(8,128)S(1)} custom-call(bf16[384,3456]{1,0:T(8,128)(2,1)S(1)} %get-tuple-element.196.early, bf16[3456,1152]{1,0:T(8,128)(2,1)S(1)} %get-tuple-element.195.taps, f32[384,384]{1,0:T(8,128)S(1)} %get-tuple-element.197.late), custom_call_target="tpu_custom_call" | custom-call | flops 384 | tf_op jit(solution)/shard_map/cond/branch_5_fun/pallas_call | solution.py:306
  28.5 0.0 collective-permute-done.26
  28.5 0.9 %collective-permute-start.28 = (bf16[3,2,24,384]{3,2,1,0:T(8,128)(2,1)S(1)}, bf16[3,2,24,384]{3,2,1,0:T(8,128)(2,1)S(1)}, u32[]{:S(2)}, u32[]{:S(2)}) collective-permute-start(bf16[3,2,24,384]{3,2,1,0:T(8,128)(2,1)S(1)} %pad_maximum_fusion.5.halo), channel_id=1, source_target_pairs={{0,192},{192,128},{128,64},{64,0},{1,193},{193,129},{129,65},{65,1... | collective-permute-start | bytes 331784 | tf_op jit(solution)/shard_map/cond/branch_5_fun/ppermute | solution.py:412
  29.5 0.0 collective-permute-done.29
  29.5 0.0 copy-start.24
  29.5 2.2 %branch_5_fun.6.stacked = bf16[2,384,3456]{2,1,0:T(8,128)(2,1)S(1)} custom-call(s32[1,4]{1,0:T(1,128)S(1)} %copy-done.12, s32[4]{0:T(128)S(1)} %copy-done.18, s32[1]{0:T(128)} %bitcast.50.group, bf16[768,384]{1,0:T(8,128)(2,1)S(1)} %bitcast.79, f32[384]{0:T(512)S(1)} %copy-done.5), custom_call_target="tpu_custom_call" | custom-call | flops 1019215872 | bytes 995328 | tf_op jit(solution)/shard_map/cond/branch_5_fun/pallas_call | solution.py:306
  31.7 4.1 %branch_5_fun.8.sums = f32[2,384,384]{2,1,0:T(8,128)S(1)} custom-call(bf16[2,384,3456]{2,1,0:T(8,128)(2,1)S(1)} %branch_5_fun.6.stacked, bf16[3456,1152]{1,0:T(8,128)(2,1)S(1)} %get-tuple-element.195.taps, f32[2,384,384]{2,1,0:T(8,128)S(1)} %branch_5_fun.7.own, f32[384]{0:T(512)S(1)} %copy-done.24), custom_call_target="tpu_custom_call" | custom-call | flops 3057647616 | bytes 2985984 | tf_op jit(solution)/shard_map/cond/branch_5_fun/pallas_call | solution.py:306
  35.8 0.0 collective-permute-done.28.halo_previous
  35.8 2.8 %branch_5_fun.9 = bf16[768,384]{1,0:T(8,128)(2,1)S(1)} custom-call(s32[1,4]{1,0:T(1,128)S(1)} %copy-done.12, s32[1]{0:T(128)} %get-tuple-element.187.tile_row, s32[4]{0:T(128)S(1)} %copy-done.18, s32[1]{0:T(128)} %bitcast.50.group, bf16[3,2,24,384]{3,2,1,0:T(8,128)(2,1)S(1)} %pad_maximum_fusion.5.halo, ...), custom_call_target="tpu_custom_call" | custom-call | flops 318504960 | bytes 311040 | tf_op jit(solution)/shard_map/cond/branch_5_fun/pallas_call | solution.py:306
  39.0 0.0 copy-start.6
  39.0 0.8 %copy-done.6 = bf16[1,2,16,24,384]{4,3,2,1,0:T(8,128)(2,1)} copy-done((bf16[1,2,16,24,384]{4,3,2,1,0:T(8,128)(2,1)}, bf16[1,2,16,24,384]{4,3,2,1,0:T(8,128)(2,1)S(1)}, u32[]{:S(2)}) %copy-start.6) | copy-done | bytes 589848
  (9 shorter events, 0.0 us)
Async XLA Ops:
  2.2 14.6 %collective-permute-start.25 = (bf16[2,24,384]{2,1,0:T(8,128)(2,1)S(1)}, bf16[2,24,384]{2,1,0:T(8,128)(2,1)S(1)}, u32[]{:S(2)}, u32[]{:S(2)}) collective-permute-start(bf16[2,24,384]{2,1,0:T(8,128)(2,1)S(1)} %get-tuple-element.190), channel_id=1, source_target_pairs={{0,32},{2,34},{4,36},{6,38},{8,40},{10,42},{12,44},{14,46},{16,48}... | collective-permute-start | bytes 110600 | tf_op jit(solution)/shard_map/cond/branch_5_fun/ppermute | solution.py:369
  8.6 20.8 %collective-permute-start.29 = (bf16[1,2,16,24,384]{4,3,2,1,0:T(8,128)(2,1)}, bf16[1,2,16,24,384]{4,3,2,1,0:T(8,128)(2,1)S(1)}, u32[]{:S(2)}, u32[]{:S(2)}) collective-permute-start(bf16[1,2,16,24,384]{4,3,2,1,0:T(8,128)(2,1)} %get-tuple-element.191), channel_id=1, source_target_pairs={{0,192},{192,128},{128,64},{64,0},{1,193},{193,129},{129,65},{65,1... | collective-permute-start | bytes 1769480 | tf_op jit(solution)/shard_map/cond/branch_5_fun/ppermute | solution.py:368
  17.0 11.5 %collective-permute-start.26 = (bf16[2,24,384]{2,1,0:T(8,128)(2,1)S(1)}, bf16[2,24,384]{2,1,0:T(8,128)(2,1)S(1)}, u32[]{:S(2)}, u32[]{:S(2)}) collective-permute-start(bf16[2,24,384]{2,1,0:T(8,128)(2,1)S(1)} %get-tuple-element.298), channel_id=1, source_target_pairs={{0,2},{2,4},{4,6},{6,8},{8,10},{10,12},{12,14},{14,16},{16,18},{18... | collective-permute-start | bytes 110600 | tf_op jit(solution)/shard_map/cond/branch_5_fun/ppermute | solution.py:397
  20.4 8.1 %collective-permute-start.27 = (bf16[2,24,384]{2,1,0:T(8,128)(2,1)S(1)}, bf16[2,24,384]{2,1,0:T(8,128)(2,1)S(1)}, u32[]{:S(2)}, u32[]{:S(2)}) collective-permute-start(bf16[2,24,384]{2,1,0:T(8,128)(2,1)S(1)} %get-tuple-element.299), channel_id=1, source_target_pairs={{2,0},{4,2},{6,4},{8,6},{10,8},{12,10},{14,12},{16,14},{18,16},{20... | collective-permute-start | bytes 110600 | tf_op jit(solution)/shard_map/cond/branch_5_fun/ppermute | solution.py:398
  24.9 4.5 %copy-start.5 = (f32[384]{0:T(512)S(1)}, f32[384]{0:T(512)}, u32[]{:S(2)}) copy-start(f32[384]{0:T(512)} %get-tuple-element.245.gain) | copy-start | bytes 4612 | tf_op jit(solution)/shard_map/cond
  24.9 4.5 %copy-start.12 = (s32[1,4]{1,0:T(1,128)S(1)}, s32[1,4]{1,0:T(1,128)}, u32[]{:S(2)}) copy-start(s32[1,4]{1,0:T(1,128)} %get-tuple-element.239.margins) | copy-start | bytes 52 | tf_op jit(solution)/shard_map/cond
  24.9 4.5 %copy-start.18 = (s32[4]{0:T(128)S(1)}, s32[4]{0:T(128)}, u32[]{:S(2)}) copy-start(s32[4]{0:T(128)} %get-tuple-element.188.group_slot) | copy-start | bytes 52 | tf_op jit(solution)/shard_map/cond
  28.5 7.3 %collective-permute-start.28 = (bf16[3,2,24,384]{3,2,1,0:T(8,128)(2,1)S(1)}, bf16[3,2,24,384]{3,2,1,0:T(8,128)(2,1)S(1)}, u32[]{:S(2)}, u32[]{:S(2)}) collective-permute-start(bf16[3,2,24,384]{3,2,1,0:T(8,128)(2,1)S(1)} %pad_maximum_fusion.5.halo), channel_id=1, source_target_pairs={{0,192},{192,128},{128,64},{64,0},{1,193},{193,129},{129,65},{65,1... | collective-permute-start | bytes 331784 | tf_op jit(solution)/shard_map/cond/branch_5_fun/ppermute | solution.py:412
  29.5 2.2 %copy-start.24 = (f32[384]{0:T(512)S(1)}, f32[384]{0:T(512)}, u32[]{:S(2)}) copy-start(f32[384]{0:T(512)} %get-tuple-element.257.bias) | copy-start | bytes 4612 | tf_op jit(solution)/shard_map/cond
  39.0 0.8 %copy-start.6 = (bf16[1,2,16,24,384]{4,3,2,1,0:T(8,128)(2,1)}, bf16[1,2,16,24,384]{4,3,2,1,0:T(8,128)(2,1)S(1)}, u32[]{:S(2)}) copy-start(bf16[1,2,16,24,384]{4,3,2,1,0:T(8,128)(2,1)S(1)} %get-tuple-element.330) | copy-start | bytes 1769476
